TPU v7x, 32 devices: a whole 2x2x4 slice. The times are simulated.
32 devices in a mesh: slab: 8 (over y, x, core), orb: 4 (over z).
Axes of the slice: x: 2, y: 2, z: 4, core: 2. Of those that a mesh axis runs over, the one named last changes fastest.
Arguments:
- orbitals: float32 [256, 16384], P('orb', 'slab'), may hold values from -6 to 6
- cell_matrices: bfloat16 [64, 512, 512], P('slab'), as said below
- connectivity: int32 [64, 512], P('slab'), may hold values from 0 to 2559, as said below
- face_lower: int32 [2048], P('slab'), may hold values from 0 to 2047, as said below
- face_upper: int32 [2048], P('slab'), may hold values from 0 to 2047, as said below
Outputs:
- orthonormal_orbitals: float32 [256, 16384], P('orb', 'slab')
Inputs may be any that keep to these rules, and one draw needn't show every extreme that they name: `connectivity`: each row names 512 distinct positions of its slab's extended numbering. `face_lower`: each slab's block of 256 entries names distinct own nodes; it shares no entry with the same slab's block of face_upper. `face_upper`: each slab's block of 256 entries names distinct own nodes; it shares no entry with the same slab's block of face_lower. `cell_matrices`: each cell matrix is symmetric.
All inputs are finite; a program needn't handle non-finite values.
Results may differ from a plain program's by a relative error of at most 0.023.
Values may be sent and summed in bfloat16 or wider, within the bound.
No kernel may reach another device: no remote copies, remote signals or barrier semaphores. Data moves between devices by JAX's collectives and lax.ppermute only.
A program may use at most 64 MiB of HBM per device.

v0:
```python
import functools
import math

import jax
import jax.numpy as jnp
from jax import lax
from jax.experimental import pallas as pl
from jax.experimental.pallas import tpu as pltpu
from jax.sharding import PartitionSpec as P

DEGREE = 4
LANES = 128
SUBLANES = 8
CHUNK = LANES * SUBLANES
PITCH = SUBLANES + 1


def assemble_kernel(rows_ref, column_ref, nodes_ref, cell_ref, out_ref, total, terms):
    cell = pl.program_id(1)
    cell_nodes = cell_ref.shape[1]
    ext_count = out_ref.shape[0]

    @pl.when(cell == 0)
    def _():
        total[...] = jnp.zeros_like(total)

    picker = (nodes_ref[0] == column_ref[...]).astype(jnp.float32).astype(jnp.bfloat16)
    for pair in range(CHUNK // 256):
        spread = jnp.dot(
            cell_ref[0], picker[:, pair * 256 : (pair + 1) * 256], preferred_element_type=jnp.float32
        )
        for first in range(0, cell_nodes, SUBLANES):
            for half in range(2):
                terms[pl.ds(first * PITCH + 2 * pair + half, SUBLANES, stride=PITCH), :] = spread[
                    first : first + SUBLANES, half * LANES : (half + 1) * LANES
                ]

    group = 16

    def add_rows(step, carry):
        first = step * group
        places = [rows_ref[cell * cell_nodes + first + k] * PITCH for k in range(group)]
        sums = [
            total[pl.ds(places[k], SUBLANES), :] + terms[pl.ds((first + k) * PITCH, SUBLANES), :]
            for k in range(group)
        ]
        for k in range(group):
            total[pl.ds(places[k], SUBLANES), :] = sums[k]
        return carry

    lax.fori_loop(0, cell_nodes // group, add_rows, 0)

    @pl.when(cell == pl.num_programs(1) - 1)
    def _():
        def write_rows(step, carry):
            first = pl.multiple_of(step * 16, 16)
            for block in range(SUBLANES):
                upper = total[pl.ds(first * PITCH + block, SUBLANES, stride=PITCH), :]
                lower = total[pl.ds((first + 8) * PITCH + block, SUBLANES, stride=PITCH), :]
                out_ref[pl.ds(first, 16), block * LANES : (block + 1) * LANES] = jnp.concatenate(
                    [upper, lower], axis=0
                ).astype(jnp.bfloat16)
            return carry

        lax.fori_loop(0, ext_count // 16, write_rows, 0)


def assemble(rows, columns, connectivity, cell_matrices, ext_count):
    cells, cell_nodes, _ = cell_matrices.shape
    chunks = columns.shape[0] // CHUNK
    return pl.pallas_call(
        assemble_kernel,
        out_shape=jax.ShapeDtypeStruct((ext_count, columns.shape[0]), jnp.bfloat16),
        grid_spec=pltpu.PrefetchScalarGridSpec(
            num_scalar_prefetch=1,
            grid=(chunks, cells),
            in_specs=[
                pl.BlockSpec((1, CHUNK), lambda q, c, rows: (0, q)),
                pl.BlockSpec((1, cell_nodes, 1), lambda q, c, rows: (c, 0, 0)),
                pl.BlockSpec((1, cell_nodes, cell_nodes), lambda q, c, rows: (c, 0, 0)),
            ],
            out_specs=pl.BlockSpec((ext_count, CHUNK), lambda q, c, rows: (0, q)),
            scratch_shapes=[
                pltpu.VMEM((ext_count * PITCH, LANES), jnp.float32),
                pltpu.VMEM((cell_nodes * PITCH, LANES), jnp.float32),
            ],
        ),
        compiler_params=pltpu.CompilerParams(vmem_limit_bytes=48 * 1024 * 1024),
        cost_estimate=pl.CostEstimate(
            flops=2 * cells * cell_nodes * cell_nodes * columns.shape[0],
            bytes_accessed=chunks * cells * cell_nodes * cell_nodes * 2 + ext_count * columns.shape[0] * 2,
            transcendentals=0,
        ),
    )(rows, columns[None, :], connectivity[:, :, None], cell_matrices)


def exact(left, right, contract):
    return lax.dot_general(
        left,
        right,
        (contract, ((), ())),
        precision=lax.Precision.HIGHEST,
        preferred_element_type=jnp.float32,
    )


def inverse_factor(block):
    size = block.shape[0]
    groups = size // SUBLANES
    row = lax.broadcasted_iota(jnp.int32, (SUBLANES, LANES), 0)
    lane = lax.broadcasted_iota(jnp.int32, (SUBLANES, LANES), 1)
    left = [block[g * SUBLANES : (g + 1) * SUBLANES, :] for g in range(groups)]
    right = [(lane == row + g * SUBLANES).astype(jnp.float32) for g in range(groups)]

    def over_rows(values, index):
        return jnp.broadcast_to(values[index : index + 1, :], (SUBLANES, LANES))

    for k in range(groups):
        later = range(k, groups)
        column = {
            g: [
                jnp.broadcast_to(
                    left[g][:, k * SUBLANES + q : k * SUBLANES + q + 1], (SUBLANES, LANES)
                )
                for q in range(SUBLANES)
            ]
            for g in later
        }
        for q in range(SUBLANES):
            scale = lax.rsqrt(over_rows(column[k][q], q))
            factor = {g: column[g][q] * scale for g in later}
            left_row = over_rows(left[k], q) * scale
            right_row = over_rows(right[k], q) * scale
            below = jnp.where(row > q, factor[k], 0.0)
            left[k] = jnp.where(row == q, left_row, left[k] - below * left_row)
            right[k] = jnp.where(row == q, right_row, right[k] - below * right_row)
            for other in range(q + 1, SUBLANES):
                weight = over_rows(factor[k], other)
                for g in later:
                    column[g][other] = column[g][other] - factor[g] * weight
            for g in range(k + 1, groups):
                left[g] = left[g] - factor[g] * left_row
                right[g] = right[g] - factor[g] * right_row
    return jnp.concatenate(right, axis=0)


def orthonormal_kernel(scale, block_ref, gram_ref, filtered_ref, out_ref, inverse):
    size = gram_ref.shape[0]
    count = size // LANES
    at = [slice(i * LANES, (i + 1) * LANES) for i in range(count)]
    lower = {}
    inverses = {}
    for i in range(count):
        diagonal = gram_ref[at[i], at[i]]
        for j in range(i):
            diagonal = diagonal - exact(lower[i, j], lower[i, j], ((1,), (1,)))
        inverses[i, i] = inverse_factor(diagonal)
        for k in range(i + 1, count):
            entry = gram_ref[at[k], at[i]]
            for j in range(i):
                entry = entry - exact(lower[k, j], lower[i, j], ((1,), (1,)))
            lower[k, i] = exact(entry, inverses[i, i], ((1,), (1,)))
    inverse[...] = jnp.zeros_like(inverse)
    for i in range(count):
        for j in range(i):
            entry = exact(lower[i, j], inverses[j, j], ((1,), (0,)))
            for m in range(j + 1, i):
                entry = entry + exact(lower[i, m], inverses[m, j], ((1,), (0,)))
            inverses[i, j] = -exact(inverses[i, i], entry, ((1,), (0,)))
            inverse[at[i], at[j]] = inverses[i, j] * scale
        inverse[at[i], at[i]] = inverses[i, i] * scale
    rows = out_ref.shape[0]
    mine = inverse[pl.ds(pl.multiple_of(block_ref[0] * rows, rows), rows), :]
    high = mine.astype(jnp.bfloat16)
    low = (mine - high.astype(jnp.float32)).astype(jnp.bfloat16)
    width = 512
    for first in range(0, out_ref.shape[1], width):
        part = filtered_ref[:, first : first + width]
        out_ref[:, first : first + width] = jnp.dot(
            high, part, preferred_element_type=jnp.float32
        ) + jnp.dot(low, part, preferred_element_type=jnp.float32)


def orthonormal(block, gram, filtered, rows, scale):
    size = gram.shape[0]
    return pl.pallas_call(
        functools.partial(orthonormal_kernel, scale),
        out_shape=jax.ShapeDtypeStruct((rows, filtered.shape[1]), jnp.float32),
        in_specs=[
            pl.BlockSpec(memory_space=pltpu.SMEM),
            pl.BlockSpec(memory_space=pltpu.VMEM),
            pl.BlockSpec(memory_space=pltpu.VMEM),
        ],
        out_specs=pl.BlockSpec(memory_space=pltpu.VMEM),
        scratch_shapes=[pltpu.VMEM((size, size), jnp.float32)],
        compiler_params=pltpu.CompilerParams(vmem_limit_bytes=16 * 1024 * 1024),
    )(block, gram, filtered)


def swap_pairs(count, first):
    pairs = []
    for low in range(first, count - 1, 2):
        pairs += [(low, low + 1), (low + 1, low)]
    return pairs


def sum_over(values, axis):
    count = lax.axis_size(axis)
    if count & (count - 1):
        return lax.psum(values.astype(jnp.bfloat16), axis).astype(jnp.float32)
    step = 1
    while step < count:
        sent = values.astype(jnp.bfloat16)
        got = lax.ppermute(sent, axis, [(i, i ^ step) for i in range(count)])
        values = sent.astype(jnp.float32) + got.astype(jnp.float32)
        step *= 2
    return values


def per_device(orbitals, cell_matrices, connectivity, face_lower, face_upper):
    own_count = orbitals.shape[1]
    face = face_lower.shape[0]
    ext_count = own_count + 2 * face
    slabs = lax.axis_size("slab")
    slab = lax.axis_index("slab")
    even = slab % 2 == 0

    gathered = lax.all_gather(orbitals.astype(jnp.bfloat16), "orb", axis=0, tiled=True)

    has_lower = slab > 0
    has_upper = slab < slabs - 1
    has_a = jnp.where(even, has_upper, has_lower)
    has_b = jnp.where(even, has_lower, has_upper)
    ghost_lower = jnp.arange(face, dtype=jnp.int32)
    ghost_upper = ghost_lower + (face + own_count)
    face_a = jnp.where(even, face_upper, face_lower)
    face_b = jnp.where(even, face_lower, face_upper)
    ghost_a = jnp.where(even, ghost_upper, ghost_lower)
    ghost_b = jnp.where(even, ghost_lower, ghost_upper)

    lower_at = jnp.where(even, own_count + face, own_count)
    upper_at = jnp.where(even, own_count, own_count + face)
    rows = jnp.where(
        connectivity < face,
        connectivity + lower_at,
        jnp.where(
            connectivity < face + own_count,
            connectivity - face,
            connectivity - (face + own_count) + upper_at,
        ),
    ).reshape(-1)
    shared_columns = jnp.concatenate([ghost_a, face_a + face, ghost_b, face_b + face])
    own_columns = jnp.arange(own_count, dtype=jnp.int32) + face

    shared_matrix = assemble(rows, shared_columns, connectivity, cell_matrices, ext_count)
    own_matrix = assemble(rows, own_columns, connectivity, cell_matrices, ext_count)

    face_nodes = jnp.concatenate([face_a, face_b])
    face_table = (
        face_nodes[:, None] == lax.broadcasted_iota(jnp.int32, (2 * face, own_count), 1)
    ).astype(jnp.bfloat16)

    pairs_a = swap_pairs(slabs, 0)
    pairs_b = swap_pairs(slabs, 1)

    def times(left, right):
        return jnp.dot(left, right, preferred_element_type=jnp.float32)

    def apply_hamiltonian(extended):
        shared = times(extended, shared_matrix)
        sent = shared.astype(jnp.bfloat16)
        got_a = lax.ppermute(sent[:, : 2 * face], "slab", pairs_a)
        got_b = lax.ppermute(sent[:, 2 * face :], "slab", pairs_b)
        own = times(extended, own_matrix)
        incoming = jnp.concatenate([got_a[:, :face], got_b[:, :face]], axis=1)
        own = own + times(incoming, face_table)
        at_a = jnp.where(has_a, shared[:, :face] + got_a[:, face:].astype(jnp.float32), 0.0)
        at_b = jnp.where(
            has_b, shared[:, 2 * face : 3 * face] + got_b[:, face:].astype(jnp.float32), 0.0
        )
        return own, at_a, at_b

    def extend(own, at_a, at_b):
        return jnp.concatenate([own, at_a, at_b], axis=1).astype(jnp.bfloat16)

    faces = lax.dot_general(
        gathered, face_table, (((1,), (1,)), ((), ())), preferred_element_type=jnp.float32
    ).astype(jnp.bfloat16)
    ghosts_a = lax.ppermute(faces[:, :face], "slab", pairs_a)
    ghosts_b = lax.ppermute(faces[:, face:], "slab", pairs_b)
    start = jnp.concatenate([gathered, ghosts_a, ghosts_b], axis=1)
    previous = tuple(x.astype(jnp.float32) for x in (gathered, ghosts_a, ghosts_b))
    current = apply_hamiltonian(start)
    for degree_step in range(1, DEGREE):
        product = apply_hamiltonian(extend(*current))
        following = tuple(2.0 * p - q for p, q in zip(product, previous))
        previous, current = current, following

    filtered = current[0].astype(jnp.bfloat16)
    gram = lax.dot_general(
        filtered, filtered, (((1,), (1,)), ((), ())), preferred_element_type=jnp.float32
    )
    total = sum_over(gram, "slab")
    block = lax.axis_index("orb").astype(jnp.int32).reshape(1)
    return orthonormal(block, total, filtered, orbitals.shape[0], math.sqrt(own_count * slabs))


def solution(mesh):
    in_specs = (P("orb", "slab"), P("slab", None, None), P("slab", None), P("slab"), P("slab"))
    out_specs = P("orb", "slab")
    return jax.shard_map(
        per_device, mesh=mesh, in_specs=in_specs, out_specs=out_specs, check_vma=False
    )
```

profile of v0, /device:TPU:0, one launch (start us, length us, event | category | flops | bytes accessed | tf_op | source)
XLA Modules:
  0.0 176.2 jit_solution(12529261088637754991)
XLA Ops:
  6.5 1.8 %convert_element_type.82 = bf16[64,2048]{1,0:T(8,128)(2,1)} convert(f32[64,2048]{1,0:T(8,128)} %param.5) | non-fusion elementwise | flops 131072 | bytes 786432 | tf_op jit(solution)/shard_map/convert_element_type | solution.py:228
  9.1 1.4 copy.8.nodes_ref
  10.6 20.6 %shard_map.56 = bf16[2560,1024]{1,0:T(8,128)(2,1)} custom-call(s32[4096]{0:T(1024)S(1)} %bitcast.21, s32[1,1024]{1,0:T(1,128)S(1)} %bitcast.23, s32[8,512,1]{2,1,0:T(8,128)S(1)} %copy.8.nodes_ref, bf16[8,512,512]{2,1,0:T(8,128)(2,1)} %cell_ref.3), custom_call_target="tpu_custom_call" | custom-call | flops 4294967296 | bytes 9437184 | tf_op jit(solution)/shard_map/pallas_call | solution.py:71
  31.2 8.4 %all-gather.2.cloned.1.call-done = bf16[256,2048]{1,0:T(8,128)(2,1)} async-done(((bf16[64,2048]{1,0:T(8,128)(2,1)}), bf16[256,2048]{1,0:T(8,128)(2,1)}) %all-gather.2.cloned.1.call-update) | async-done | bytes 1048592 | tf_op jit(solution)/shard_map/all_gather | solution.py:228
  39.6 2.4 %fusion.22 = bf16[256,512]{1,0:T(8,128)(2,1)S(1)} fusion(bf16[256,2048]{1,0:T(8,128)(2,1)} %all-gather.2.cloned.1.call-done, s32[512]{0:T(512)S(1)} %pad_add_fusion.1), kind=kOutput, calls=%fused_computation.28 | convolution fusion | flops 538050560 | bytes 1312768 | tf_op jit(solution)/shard_map/dot_general | solution.py:286
  42.7 2.9 %collective-permute-start = (bf16[256,256]{1,0:T(8,128)(2,1)S(1)}, bf16[256,256]{1,0:T(8,128)(2,1)S(1)}, u32[]{:S(2)}, u32[]{:S(2)}) collective-permute-start(bf16[256,256]{1,0:T(8,128)(2,1)S(1)} %get-tuple-element.24), channel_id=1, source_target_pairs={{0,4},{4,0},{8,12},{12,8},{16,20},{20,16},{24,28},{28,24},{1,5},{5... | collective-permute-start | bytes 393224 | tf_op jit(solution)/shard_map/ppermute | solution.py:289
  47.9 2.5 %fusion.75 = (bf16[256,1024]{1,0:T(8,128)(2,1)S(1)}, f32[256,1024]{1,0:T(8,128)}) fusion(bf16[256,2560]{1,0:T(8,128)(2,1)S(1)} %constant_dynamic-update-slice_fusion, bf16[2560,1024]{1,0:T(8,128)(2,1)S(1)} %copy-done.10), kind=kOutput, calls=%fused_computation.105 | convolution fusion | flops 1342439424 | bytes 8126464 | tf_op jit(solution)/shard_map/dot_general | solution.py:267
  51.3 1.5 collective-permute-start.2
  52.8 1.4 collective-permute-start.3
  54.2 37.7 %shard_map.55 = bf16[2560,2048]{1,0:T(8,128)(2,1)} custom-call(s32[4096]{0:T(1024)S(1)} %bitcast.22, s32[1,2048]{1,0:T(1,128)S(1)} %iota_add_fusion.column_ref, s32[8,512,1]{2,1,0:T(8,128)S(1)} %copy.8.nodes_ref, bf16[8,512,512]{2,1,0:T(8,128)(2,1)} %cell_ref.3), custom_call_target="tpu_custom_call" | custom-call | flops 8589934592 | bytes 18874368 | tf_op jit(solution)/shard_map/pallas_call | solution.py:71
  92.9 1.0 fusion.3
  94.0 6.1 %fusion.76 = (bf16[256,2048]{1,0:T(8,128)(2,1)S(1)}, f32[256,2048]{1,0:T(8,128)S(1)}) fusion(f32[256,2048]{1,0:T(8,128)S(1)} %fusion.3, bf16[256,2560]{1,0:T(8,128)(2,1)S(1)} %copy-done.3, bf16[2560,2048]{1,0:T(8,128)(2,1)} %shard_map.55), kind=kOutput, calls=%fused_computation.106 | convolution fusion | flops 2685403136 | bytes 17039360 | tf_op jit(solution)/shard_map/dot_general | solution.py:267
  100.1 1.7 fusion.58
  101.8 1.5 fusion.77
  103.4 3.7 %collective-permute-start.4 = (bf16[256,512]{1,0:T(8,128)(2,1)S(1)}, bf16[256,512]{1,0:T(8,128)(2,1)S(1)}, u32[]{:S(2)}, u32[]{:S(2)}) collective-permute-start(bf16[256,512]{1,0:T(8,128)(2,1)S(1)} %get-tuple-element.19), channel_id=1, source_target_pairs={{0,4},{4,0},{8,12},{12,8},{16,20},{20,16},{24,28},{28,24},{1,5},{5... | collective-permute-start | bytes 786440 | tf_op jit(solution)/shard_map/ppermute | solution.py:272
  108.1 2.9 %fusion.27 = f32[256,2048]{1,0:T(8,128)S(1)} fusion(bf16[2560,2048]{1,0:T(8,128)(2,1)S(1)} %bitcast.28, bf16[256,256]{1,0:T(8,128)(2,1)S(1)} %get-tuple-element.14, bf16[256,256]{1,0:T(8,128)(2,1)S(1)} %get-tuple-element.13, bf16[256,2048]{1,0:T(8,128)(2,1)S(1)} %get-tuple-element.29), kind=kOutput, calls=%fused_computation.34 | convolution fusion | flops 2688286720 | bytes 13893632 | tf_op jit(solution)/shard_map/dot_general | solution.py:267
  111.3 1.3 fusion.78
  112.5 1.5 fusion.79
  114.1 6.5 %collective-permute-start.6 = (bf16[256,512]{1,0:T(8,128)(2,1)S(1)}, bf16[256,512]{1,0:T(8,128)(2,1)S(1)}, u32[]{:S(2)}, u32[]{:S(2)}) collective-permute-start(bf16[256,512]{1,0:T(8,128)(2,1)S(1)} %get-tuple-element.17), channel_id=1, source_target_pairs={{0,4},{4,0},{8,12},{12,8},{16,20},{20,16},{24,28},{28,24},{1,5},{5... | collective-permute-start | bytes 786440 | tf_op jit(solution)/shard_map/ppermute | solution.py:272
  121.3 2.9 %fusion.25 = f32[256,2048]{1,0:T(8,128)S(1)} fusion(bf16[2560,2048]{1,0:T(8,128)(2,1)S(1)} %bitcast.28, bf16[256,256]{1,0:T(8,128)(2,1)S(1)} %get-tuple-element.12, bf16[256,256]{1,0:T(8,128)(2,1)S(1)} %get-tuple-element.11, bf16[256,2048]{1,0:T(8,128)(2,1)S(1)} %get-tuple-element.33), kind=kOutput, calls=%fused_computation.32 | convolution fusion | flops 2688286720 | bytes 13893632 | tf_op jit(solution)/shard_map/dot_general | solution.py:267
  124.3 1.3 fusion.14
  125.6 1.1 fusion.35
  126.7 1.5 convolution_convert_fusion
  128.3 5.8 %collective-permute-start.8 = (bf16[256,512]{1,0:T(8,128)(2,1)S(1)}, bf16[256,512]{1,0:T(8,128)(2,1)S(1)}, u32[]{:S(2)}, u32[]{:S(2)}) collective-permute-start(bf16[256,512]{1,0:T(8,128)(2,1)S(1)} %get-tuple-element.15), channel_id=1, source_target_pairs={{0,4},{4,0},{8,12},{12,8},{16,20},{20,16},{24,28},{28,24},{1,5},{5... | collective-permute-start | bytes 786440 | tf_op jit(solution)/shard_map/ppermute | solution.py:272
  135.0 2.9 %fusion.23 = f32[256,2048]{1,0:T(8,128)S(1)} fusion(bf16[2560,2048]{1,0:T(8,128)(2,1)S(1)} %bitcast.28, bf16[256,256]{1,0:T(8,128)(2,1)S(1)} %get-tuple-element.10, bf16[256,256]{1,0:T(8,128)(2,1)S(1)} %get-tuple-element.9, bf16[256,2048]{1,0:T(8,128)(2,1)S(1)} %fusion.14), kind=kOutput, calls=%fused_computation.30 | convolution fusion | flops 2688286720 | bytes 13893632 | tf_op jit(solution)/shard_map/dot_general | solution.py:267
  138.0 1.3 fusion.15.filtered_ref
  139.7 6.7 %collective-permute-start.10 = (bf16[256,256]{1,0:T(8,128)(2,1)S(1)}, bf16[256,256]{1,0:T(8,128)(2,1)S(1)}, u32[]{:S(2)}, u32[]{:S(2)}) collective-permute-start(bf16[256,256]{1,0:T(8,128)(2,1)S(1)} %convolution_convert_fusion.1), channel_id=1, source_target_pairs={{0,4},{4,0},{8,12},{12,8},{16,20},{20,16},{24,28},{28,24},{1,5},{5... | collective-permute-start | bytes 393224 | tf_op jit(solution)/shard_map/ppermute | solution.py:214
  147.4 2.5 %collective-permute-start.11 = (bf16[256,256]{1,0:T(8,128)(2,1)S(1)}, bf16[256,256]{1,0:T(8,128)(2,1)S(1)}, u32[]{:S(2)}, u32[]{:S(2)}) collective-permute-start(bf16[256,256]{1,0:T(8,128)(2,1)S(1)} %add_convert_fusion.1), channel_id=1, source_target_pairs={{0,8},{4,12},{8,0},{12,4},{16,24},{20,28},{24,16},{28,20},{1,9},{5... | collective-permute-start | bytes 393224 | tf_op jit(solution)/shard_map/ppermute | solution.py:214
  149.9 4.0 %collective-permute-done.11 = bf16[256,256]{1,0:T(8,128)(2,1)S(1)} collective-permute-done((bf16[256,256]{1,0:T(8,128)(2,1)S(1)}, bf16[256,256]{1,0:T(8,128)(2,1)S(1)}, u32[]{:S(2)}, u32[]{:S(2)}) %collective-permute-start.11) | collective-permute-done | bytes 131104 | tf_op jit(solution)/shard_map/ppermute | solution.py:214
  154.0 2.2 %collective-permute-start.12 = (bf16[256,256]{1,0:T(8,128)(2,1)S(1)}, bf16[256,256]{1,0:T(8,128)(2,1)S(1)}, u32[]{:S(2)}, u32[]{:S(2)}) collective-permute-start(bf16[256,256]{1,0:T(8,128)(2,1)S(1)} %add_convert_fusion), channel_id=1, source_target_pairs={{0,16},{4,20},{8,24},{12,28},{16,0},{20,4},{24,8},{28,12},{1,17},{... | collective-permute-start | bytes 393224 | tf_op jit(solution)/shard_map/ppermute | solution.py:214
  156.1 3.1 %collective-permute-done.12 = bf16[256,256]{1,0:T(8,128)(2,1)S(1)} collective-permute-done((bf16[256,256]{1,0:T(8,128)(2,1)S(1)}, bf16[256,256]{1,0:T(8,128)(2,1)S(1)}, u32[]{:S(2)}, u32[]{:S(2)}) %collective-permute-start.12) | collective-permute-done | bytes 131104 | tf_op jit(solution)/shard_map/ppermute | solution.py:214
  159.3 10.1 %shard_map.57 = f32[64,2048]{1,0:T(8,128)} custom-call(s32[1]{0:T(128)} %bitcast.block_ref, f32[256,256]{1,0:T(8,128)S(1)} %convert_add_fusion.gram_ref, bf16[256,2048]{1,0:T(8,128)(2,1)S(1)} %fusion.15.filtered_ref), custom_call_target="tpu_custom_call" | custom-call | tf_op jit(solution)/shard_map/pallas_call | solution.py:186
  (79 shorter events, 10.0 us)
Async XLA Ops:
  6.5 4.0 %copy-start.8 = (s32[256]{0:T(256)S(1)}, s32[256]{0:T(256)}, u32[]{:S(2)}) copy-start(s32[256]{0:T(256)} %param.9) | copy-start | bytes 3076
  6.5 4.0 %copy-start.9 = (s32[256]{0:T(256)S(1)}, s32[256]{0:T(256)}, u32[]{:S(2)}) copy-start(s32[256]{0:T(256)} %param.8) | copy-start | bytes 3076
  6.5 33.1 %all-gather.2.cloned.1.call-start = ((), (), s32[]{:S(2)}) async-start(), calls=%async_computation | async-start | bytes 1310720 | tf_op jit(solution)/shard_map/all_gather | solution.py:228
  39.6 6.0 %copy-start = (bf16[256,2048]{1,0:T(8,128)(2,1)S(1)}, bf16[256,2048]{1,0:T(8,128)(2,1)}, u32[]{:S(2)}) copy-start(bf16[256,2048]{1,0:T(8,128)(2,1)} %all-gather.2.cloned.1.call-done) | copy-start | bytes 3145732
  39.6 8.3 %copy-start.10 = (bf16[2560,1024]{1,0:T(8,128)(2,1)S(1)}, bf16[2560,1024]{1,0:T(8,128)(2,1)}, u32[]{:S(2)}) copy-start(bf16[2560,1024]{1,0:T(8,128)(2,1)} %shard_map.56) | copy-start | bytes 15728644
  42.1 4.6 %collective-permute-start.1 = (bf16[256,256]{1,0:T(8,128)(2,1)S(1)}, bf16[256,256]{1,0:T(8,128)(2,1)S(1)}, u32[]{:S(2)}, u32[]{:S(2)}) collective-permute-start(bf16[256,256]{1,0:T(8,128)(2,1)S(1)} %get-tuple-element.23), channel_id=1, source_target_pairs={{4,8},{8,4},{12,16},{16,12},{20,24},{24,20},{5,9},{9,5},{13,17},{1... | collective-permute-start | bytes 393224 | tf_op jit(solution)/shard_map/ppermute | solution.py:290
  42.7 3.9 %collective-permute-start = (bf16[256,256]{1,0:T(8,128)(2,1)S(1)}, bf16[256,256]{1,0:T(8,128)(2,1)S(1)}, u32[]{:S(2)}, u32[]{:S(2)}) collective-permute-start(bf16[256,256]{1,0:T(8,128)(2,1)S(1)} %get-tuple-element.24), channel_id=1, source_target_pairs={{0,4},{4,0},{8,12},{12,8},{16,20},{20,16},{24,28},{28,24},{1,5},{5... | collective-permute-start | bytes 393224 | tf_op jit(solution)/shard_map/ppermute | solution.py:289
  46.6 0.6 copy-start.6
  47.2 0.7 copy-start.4
  47.9 2.5 %copy-start.2 = (bf16[256,2560]{1,0:T(8,128)(2,1)}, bf16[256,2560]{1,0:T(8,128)(2,1)S(1)}, u32[]{:S(2)}) copy-start(bf16[256,2560]{1,0:T(8,128)(2,1)S(1)} %constant_dynamic-update-slice_fusion) | copy-start | bytes 3932164
  51.3 40.6 %collective-permute-start.2 = (bf16[256,512]{1,0:T(8,128)(2,1)}, bf16[256,512]{1,0:T(8,128)(2,1)S(1)}, u32[]{:S(2)}, u32[]{:S(2)}) collective-permute-start(bf16[256,512]{1,0:T(8,128)(2,1)} %get-tuple-element.21), channel_id=1, source_target_pairs={{0,4},{4,0},{8,12},{12,8},{16,20},{20,16},{24,28},{28,24},{1,5},{5... | collective-permute-start | bytes 786440 | tf_op jit(solution)/shard_map/ppermute | solution.py:272
  52.8 39.1 %collective-permute-start.3 = (bf16[256,512]{1,0:T(8,128)(2,1)}, bf16[256,512]{1,0:T(8,128)(2,1)}, u32[]{:S(2)}, u32[]{:S(2)}) collective-permute-start(bf16[256,512]{1,0:T(8,128)(2,1)} %get-tuple-element.22), channel_id=1, source_target_pairs={{4,8},{8,4},{12,16},{16,12},{20,24},{24,20},{5,9},{9,5},{13,17},{1... | collective-permute-start | bytes 786440 | tf_op jit(solution)/shard_map/ppermute | solution.py:273
  91.9 2.1 %copy-start.3 = (bf16[256,2560]{1,0:T(8,128)(2,1)S(1)}, bf16[256,2560]{1,0:T(8,128)(2,1)}, u32[]{:S(2)}) copy-start(bf16[256,2560]{1,0:T(8,128)(2,1)} %copy-done.2) | copy-start | bytes 3932164
  92.9 8.9 %slice-start = ((s8[5242880]{0:T(1024)(128)(4,1)}), s8[4194304]{0:T(1024)(128)(4,1)S(1)}, s32[]{:S(2)}) async-start(s8[5242880]{0:T(1024)(128)(4,1)} %bitcast.25), calls=%async_computation.1 | async-start | bytes 8388608
  92.9 15.1 %slice-start.2 = ((s8[10485760]{0:T(1024)(128)(4,1)}), s8[4194304]{0:T(1024)(128)(4,1)S(1)}, s32[]{:S(2)}) async-start(s8[10485760]{0:T(1024)(128)(4,1)} %bitcast.27), calls=%async_computation.3 | async-start | bytes 8388608
  94.0 6.1 %copy-start.1 = (f32[256,1024]{1,0:T(8,128)S(1)}, f32[256,1024]{1,0:T(8,128)}, u32[]{:S(2)}) copy-start(f32[256,1024]{1,0:T(8,128)} %get-tuple-element.28) | copy-start | bytes 3145732
  94.0 7.8 %slice-start.1 = ((s8[5242880]{0:T(1024)(128)(4,1)}), s8[1048576]{0:T(1024)(128)(4,1)S(1)}, s32[]{:S(2)}) async-start(s8[5242880]{0:T(1024)(128)(4,1)} %bitcast.25), calls=%async_computation.2 | async-start | bytes 2097152
  94.0 14.1 %slice-start.3 = ((s8[10485760]{0:T(1024)(128)(4,1)}), s8[4194304]{0:T(1024)(128)(4,1)S(1)}, s32[]{:S(2)}) async-start(s8[10485760]{0:T(1024)(128)(4,1)} %bitcast.27), calls=%async_computation.4 | async-start | bytes 8388608
  94.0 14.1 %slice-start.4 = ((s8[10485760]{0:T(1024)(128)(4,1)}), s8[2097152]{0:T(1024)(128)(4,1)S(1)}, s32[]{:S(2)}) async-start(s8[10485760]{0:T(1024)(128)(4,1)} %bitcast.27), calls=%async_computation.5 | async-start | bytes 4194304
  103.4 7.6 %collective-permute-start.4 = (bf16[256,512]{1,0:T(8,128)(2,1)S(1)}, bf16[256,512]{1,0:T(8,128)(2,1)S(1)}, u32[]{:S(2)}, u32[]{:S(2)}) collective-permute-start(bf16[256,512]{1,0:T(8,128)(2,1)S(1)} %get-tuple-element.19), channel_id=1, source_target_pairs={{0,4},{4,0},{8,12},{12,8},{16,20},{20,16},{24,28},{28,24},{1,5},{5... | collective-permute-start | bytes 786440 | tf_op jit(solution)/shard_map/ppermute | solution.py:272
  107.1 4.0 %copy-start.5 = (bf16[256,256]{1,0:T(8,128)(2,1)S(1)}, bf16[256,256]{1,0:T(8,128)(2,1)}, u32[]{:S(2)}) copy-start(bf16[256,256]{1,0:T(8,128)(2,1)} %copy-done.4) | copy-start | bytes 393220
  107.1 4.0 %copy-start.7 = (bf16[256,256]{1,0:T(8,128)(2,1)S(1)}, bf16[256,256]{1,0:T(8,128)(2,1)}, u32[]{:S(2)}) copy-start(bf16[256,256]{1,0:T(8,128)(2,1)} %copy-done.6) | copy-start | bytes 393220
  107.1 4.0 %collective-permute-start.5 = (bf16[256,512]{1,0:T(8,128)(2,1)S(1)}, bf16[256,512]{1,0:T(8,128)(2,1)S(1)}, u32[]{:S(2)}, u32[]{:S(2)}) collective-permute-start(bf16[256,512]{1,0:T(8,128)(2,1)S(1)} %get-tuple-element.20), channel_id=1, source_target_pairs={{4,8},{8,4},{12,16},{16,12},{20,24},{24,20},{5,9},{9,5},{13,17},{1... | collective-permute-start | bytes 786440 | tf_op jit(solution)/shard_map/ppermute | solution.py:273
  114.1 10.1 %collective-permute-start.6 = (bf16[256,512]{1,0:T(8,128)(2,1)S(1)}, bf16[256,512]{1,0:T(8,128)(2,1)S(1)}, u32[]{:S(2)}, u32[]{:S(2)}) collective-permute-start(bf16[256,512]{1,0:T(8,128)(2,1)S(1)} %get-tuple-element.17), channel_id=1, source_target_pairs={{0,4},{4,0},{8,12},{12,8},{16,20},{20,16},{24,28},{28,24},{1,5},{5... | collective-permute-start | bytes 786440 | tf_op jit(solution)/shard_map/ppermute | solution.py:272
  120.6 3.6 %collective-permute-start.7 = (bf16[256,512]{1,0:T(8,128)(2,1)S(1)}, bf16[256,512]{1,0:T(8,128)(2,1)S(1)}, u32[]{:S(2)}, u32[]{:S(2)}) collective-permute-start(bf16[256,512]{1,0:T(8,128)(2,1)S(1)} %get-tuple-element.18), channel_id=1, source_target_pairs={{4,8},{8,4},{12,16},{16,12},{20,24},{24,20},{5,9},{9,5},{13,17},{1... | collective-permute-start | bytes 786440 | tf_op jit(solution)/shard_map/ppermute | solution.py:273
  128.3 9.6 %collective-permute-start.8 = (bf16[256,512]{1,0:T(8,128)(2,1)S(1)}, bf16[256,512]{1,0:T(8,128)(2,1)S(1)}, u32[]{:S(2)}, u32[]{:S(2)}) collective-permute-start(bf16[256,512]{1,0:T(8,128)(2,1)S(1)} %get-tuple-element.15), channel_id=1, source_target_pairs={{0,4},{4,0},{8,12},{12,8},{16,20},{20,16},{24,28},{28,24},{1,5},{5... | collective-permute-start | bytes 786440 | tf_op jit(solution)/shard_map/ppermute | solution.py:272
  134.1 3.9 %collective-permute-start.9 = (bf16[256,512]{1,0:T(8,128)(2,1)S(1)}, bf16[256,512]{1,0:T(8,128)(2,1)S(1)}, u32[]{:S(2)}, u32[]{:S(2)}) collective-permute-start(bf16[256,512]{1,0:T(8,128)(2,1)S(1)} %get-tuple-element.16), channel_id=1, source_target_pairs={{4,8},{8,4},{12,16},{16,12},{20,24},{24,20},{5,9},{9,5},{13,17},{1... | collective-permute-start | bytes 786440 | tf_op jit(solution)/shard_map/ppermute | solution.py:273
  139.7 7.6 %collective-permute-start.10 = (bf16[256,256]{1,0:T(8,128)(2,1)S(1)}, bf16[256,256]{1,0:T(8,128)(2,1)S(1)}, u32[]{:S(2)}, u32[]{:S(2)}) collective-permute-start(bf16[256,256]{1,0:T(8,128)(2,1)S(1)} %convolution_convert_fusion.1), channel_id=1, source_target_pairs={{0,4},{4,0},{8,12},{12,8},{16,20},{20,16},{24,28},{28,24},{1,5},{5... | collective-permute-start | bytes 393224 | tf_op jit(solution)/shard_map/ppermute | solution.py:214
  147.4 6.5 %collective-permute-start.11 = (bf16[256,256]{1,0:T(8,128)(2,1)S(1)}, bf16[256,256]{1,0:T(8,128)(2,1)S(1)}, u32[]{:S(2)}, u32[]{:S(2)}) collective-permute-start(bf16[256,256]{1,0:T(8,128)(2,1)S(1)} %add_convert_fusion.1), channel_id=1, source_target_pairs={{0,8},{4,12},{8,0},{12,4},{16,24},{20,28},{24,16},{28,20},{1,9},{5... | collective-permute-start | bytes 393224 | tf_op jit(solution)/shard_map/ppermute | solution.py:214
  154.0 5.3 %collective-permute-start.12 = (bf16[256,256]{1,0:T(8,128)(2,1)S(1)}, bf16[256,256]{1,0:T(8,128)(2,1)S(1)}, u32[]{:S(2)}, u32[]{:S(2)}) collective-permute-start(bf16[256,256]{1,0:T(8,128)(2,1)S(1)} %add_convert_fusion), channel_id=1, source_target_pairs={{0,16},{4,20},{8,24},{12,28},{16,0},{20,4},{24,8},{28,12},{1,17},{... | collective-permute-start | bytes 393224 | tf_op jit(solution)/shard_map/ppermute | solution.py:214
Sparse Core Ops, SparseCore 0:
  8.9 30.6 all-gather.1
where the time goes:
time: 177 us; the launch traced here: 176 us
  Pallas kernels  68.4 us (39%)
  starting transfers between devices  36.3 us (21%)
  matrix products  29.7 us (17%)
  waiting for transfers between devices  17.4 us (10%)
  between operations  13.9 us (8%)
  other arithmetic  5.58 us (3%)
  local copies, waits for them, and re-layouts  4.83 us (3%)
    pallas_call x2, Pallas kernels, assemble(): pl.pallas_call(assemble_kernel, out_shape=jax.ShapeDtypeStruct((ext_count...  58.3 us
    dot_general x12, matrix products, times(): return jnp.dot(left, right, preferred_element_type=jnp.float32)  26.8 us
    ppermute x4, starting transfers between devices, apply_hamiltonian(): got_a = lax.ppermute(sent[:, :2 * face], 'slab', pairs_a)  17.4 us
    ppermute x3, starting transfers between devices, sum_over(): got = lax.ppermute(sent, axis, [(i, i ^ step) for i in range(count)])  11.4 us
    pallas_call x1, Pallas kernels, orthonormal(): pl.pallas_call(functools.partial(orthonormal_kernel, scale), out_shape=ja...  10.1 us
    all_gather x1, waiting for transfers between devices, per_device(): lax.all_gather(orbitals.astype(jnp.bfloat16), 'orb', axis=0, tiled=True)  8.4 us
    ppermute x3, waiting for transfers between devices, sum_over(): got = lax.ppermute(sent, axis, [(i, i ^ step) for i in range(count)])  8.08 us
    ppermute x4, starting transfers between devices, apply_hamiltonian(): got_b = lax.ppermute(sent[:, 2 * face:], 'slab', pairs_b)  3.91 us
  transfers between devices with their start and end apart: 14, of which 5 were waited for; matrix products, arithmetic and copies ran while one was open for 6% of the time, Pallas kernels for 33%

commit v1 on v0

--- a/solution.py
+++ b/solution.py
@@ -15,42 +15,82 @@
 PITCH = SUBLANES + 1
 
 
-def assemble_kernel(rows_ref, column_ref, nodes_ref, cell_ref, out_ref, total, terms):
+def assemble_kernel(places_ref, column_ref, nodes_ref, cell_ref, out_ref, total, even_terms, odd_terms):
     cell = pl.program_id(1)
+    cells = pl.num_programs(1)
     cell_nodes = cell_ref.shape[1]
     ext_count = out_ref.shape[0]
+    parts = CHUNK // 256
+    part_rows = cell_nodes // parts
+    group = 32
+
+    def spread_part(part):
+        columns = column_ref[:, pl.ds(pl.multiple_of(part * 256, 256), 256)]
+        picker = jnp.concatenate(
+            [
+                (nodes_ref[0] == columns[:, half * LANES : (half + 1) * LANES])
+                .astype(jnp.float32)
+                .astype(jnp.bfloat16)
+                for half in range(2)
+            ],
+            axis=1,
+        )
+        return jnp.dot(cell_ref[0], picker, preferred_element_type=jnp.float32)
+
+    def keep_part(part, spread, terms):
+        for first in range(0, cell_nodes, SUBLANES):
+            for half in range(2):
+                terms[pl.ds(first * PITCH + 2 * part + half, SUBLANES, stride=PITCH), :] = spread[
+                    first : first + SUBLANES, half * LANES : (half + 1) * LANES
+                ]
+
+    def add_part(part, of_cell, terms):
+        first = part * part_rows
+        for start in range(0, part_rows, group):
+            places = [places_ref[of_cell * cell_nodes + first + start + k] for k in range(group)]
+            sums = [
+                total[pl.ds(places[k], SUBLANES), :]
+                + terms[pl.ds((first + start + k) * PITCH, SUBLANES), :]
+                for k in range(group)
+            ]
+            for k in range(group):
+                total[pl.ds(places[k], SUBLANES), :] = sums[k]
 
     @pl.when(cell == 0)
     def _():
-        total[...] = jnp.zeros_like(total)
-
-    picker = (nodes_ref[0] == column_ref[...]).astype(jnp.float32).astype(jnp.bfloat16)
-    for pair in range(CHUNK // 256):
-        spread = jnp.dot(
-            cell_ref[0], picker[:, pair * 256 : (pair + 1) * 256], preferred_element_type=jnp.float32
-        )
-        for first in range(0, cell_nodes, SUBLANES):
-            for half in range(2):
-                terms[pl.ds(first * PITCH + 2 * pair + half, SUBLANES, stride=PITCH), :] = spread[
-                    first : first + SUBLANES, half * LANES : (half + 1) * LANES
-                ]
-
-    group = 16
-
-    def add_rows(step, carry):
-        first = step * group
-        places = [rows_ref[cell * cell_nodes + first + k] * PITCH for k in range(group)]
-        sums = [
-            total[pl.ds(places[k], SUBLANES), :] + terms[pl.ds((first + k) * PITCH, SUBLANES), :]
-            for k in range(group)
-        ]
-        for k in range(group):
-            total[pl.ds(places[k], SUBLANES), :] = sums[k]
-        return carry
-
-    lax.fori_loop(0, cell_nodes // group, add_rows, 0)
-
-    @pl.when(cell == pl.num_programs(1) - 1)
+        zero_rows = total.shape[0] // parts
+
+        def body(part, carry):
+            spread = spread_part(part)
+            total[pl.ds(pl.multiple_of(part * zero_rows, SUBLANES), zero_rows), :] = jnp.zeros(
+                (zero_rows, LANES), jnp.float32
+            )
+            keep_part(part, spread, even_terms)
+            return carry
+
+        lax.fori_loop(0, parts, body, 0)
+
+    for parity, (before, now) in enumerate(((odd_terms, even_terms), (even_terms, odd_terms))):
+
+        @pl.when((cell > 0) & (cell % 2 == parity))
+        def _():
+            def body(part, carry):
+                spread = spread_part(part)
+                add_part(part, cell - 1, before)
+                keep_part(part, spread, now)
+                return carry
+
+            lax.fori_loop(0, parts, body, 0)
+
+        @pl.when((cell == cells - 1) & (cell % 2 == parity))
+        def _():
+            def body(part, carry):
+                add_part(part, cell, now)
+                return carry
+
+            lax.fori_loop(0, parts, body, 0)
+
+    @pl.when(cell == cells - 1)
     def _():
         def write_rows(step, carry):
             first = pl.multiple_of(step * 16, 16)
@@ -62,10 +102,10 @@
                 ).astype(jnp.bfloat16)
             return carry
 
-        lax.fori_loop(0, ext_count // 16, write_rows, 0)
-
-
-def assemble(rows, columns, connectivity, cell_matrices, ext_count):
+        lax.fori_loop(0, ext_count // 16, write_rows, 0, unroll=4)
+
+
+def assemble(places, columns, nodes, cell_matrices, ext_count):
     cells, cell_nodes, _ = cell_matrices.shape
     chunks = columns.shape[0] // CHUNK
     return pl.pallas_call(
@@ -75,13 +115,14 @@
             num_scalar_prefetch=1,
             grid=(chunks, cells),
             in_specs=[
-                pl.BlockSpec((1, CHUNK), lambda q, c, rows: (0, q)),
-                pl.BlockSpec((1, cell_nodes, 1), lambda q, c, rows: (c, 0, 0)),
-                pl.BlockSpec((1, cell_nodes, cell_nodes), lambda q, c, rows: (c, 0, 0)),
+                pl.BlockSpec((1, CHUNK), lambda q, c, places: (0, q)),
+                pl.BlockSpec((1, cell_nodes, LANES), lambda q, c, places: (c, 0, 0)),
+                pl.BlockSpec((1, cell_nodes, cell_nodes), lambda q, c, places: (c, 0, 0)),
             ],
-            out_specs=pl.BlockSpec((ext_count, CHUNK), lambda q, c, rows: (0, q)),
+            out_specs=pl.BlockSpec((ext_count, CHUNK), lambda q, c, places: (0, q)),
             scratch_shapes=[
                 pltpu.VMEM((ext_count * PITCH, LANES), jnp.float32),
+                pltpu.VMEM((cell_nodes * PITCH, LANES), jnp.float32),
                 pltpu.VMEM((cell_nodes * PITCH, LANES), jnp.float32),
             ],
         ),
@@ -91,7 +132,7 @@
             bytes_accessed=chunks * cells * cell_nodes * cell_nodes * 2 + ext_count * columns.shape[0] * 2,
             transcendentals=0,
         ),
-    )(rows, columns[None, :], connectivity[:, :, None], cell_matrices)
+    )(places, columns[None, :], nodes, cell_matrices)
 
 
 def exact(left, right, contract):
@@ -240,7 +281,7 @@
 
     lower_at = jnp.where(even, own_count + face, own_count)
     upper_at = jnp.where(even, own_count, own_count + face)
-    rows = jnp.where(
+    places = jnp.where(
         connectivity < face,
         connectivity + lower_at,
         jnp.where(
@@ -248,12 +289,13 @@
             connectivity - face,
             connectivity - (face + own_count) + upper_at,
         ),
-    ).reshape(-1)
+    ).reshape(-1) * PITCH
     shared_columns = jnp.concatenate([ghost_a, face_a + face, ghost_b, face_b + face])
     own_columns = jnp.arange(own_count, dtype=jnp.int32) + face
 
-    shared_matrix = assemble(rows, shared_columns, connectivity, cell_matrices, ext_count)
-    own_matrix = assemble(rows, own_columns, connectivity, cell_matrices, ext_count)
+    nodes = jnp.broadcast_to(connectivity[:, :, None], connectivity.shape + (LANES,))
+    shared_matrix = assemble(places, shared_columns, nodes, cell_matrices, ext_count)
+    own_matrix = assemble(places, own_columns, nodes, cell_matrices, ext_count)
 
     face_nodes = jnp.concatenate([face_a, face_b])
     face_table = (

time: 177 us -> 172 us (0.972)
  Pallas kernels: 68.4 us -> 61.6 us
  waiting for transfers between devices: 17.4 us -> 19.2 us
    pallas_call x2, Pallas kernels: 58.3 us -> 51.5 us  [assemble(): pl.pallas_call(assemble_kernel, out_shape=jax.ShapeDtypeStruct((ext_count...]
  transfers between devices with their start and end apart: 14 -> 14, of which waited for: 5 -> 5; matrix products, arithmetic and copies ran while one was open for 6% -> 7% of each run, Pallas kernels for 33% -> 30%
where the time goes in v1:
time: 172 us
  Pallas kernels  61.6 us (36%)
  starting transfers between devices  36.3 us (21%)
  matrix products  29.8 us (17%)
  waiting for transfers between devices  19.2 us (11%)
  between operations  13.9 us (8%)
  other arithmetic  6.25 us (4%)
  local copies, waits for them, and re-layouts  4.8 us (3%)
    pallas_call x2, Pallas kernels, assemble(): pl.pallas_call(assemble_kernel, out_shape=jax.ShapeDtypeStruct((ext_count...  51.5 us
    dot_general x12, matrix products, times(): return jnp.dot(left, right, preferred_element_type=jnp.float32)  26.9 us
    ppermute x4, starting transfers between devices, apply_hamiltonian(): got_a = lax.ppermute(sent[:, :2 * face], 'slab', pairs_a)  17.4 us
    ppermute x3, starting transfers between devices, sum_over(): got = lax.ppermute(sent, axis, [(i, i ^ step) for i in range(count)])  11.3 us
    all_gather x1, waiting for transfers between devices, per_device(): lax.all_gather(orbitals.astype(jnp.bfloat16), 'orb', axis=0, tiled=True)  10.2 us
    pallas_call x1, Pallas kernels, orthonormal(): pl.pallas_call(functools.partial(orthonormal_kernel, scale), out_shape=ja...  10.1 us
    ppermute x3, waiting for transfers between devices, sum_over(): got = lax.ppermute(sent, axis, [(i, i ^ step) for i in range(count)])  8.09 us
    ppermute x4, starting transfers between devices, apply_hamiltonian(): got_b = lax.ppermute(sent[:, 2 * face:], 'slab', pairs_b)  3.91 us
  transfers between devices with their start and end apart: 14, of which 5 were waited for; matrix products, arithmetic and copies ran while one was open for 7% of the time, Pallas kernels for 30%

profile of v1, /device:TPU:0, one launch (start us, length us, event | category | flops | bytes accessed | tf_op | source)
XLA Modules:
  0.0 171.8 jit_solution(13824342005414346658)
XLA Ops:
  6.5 1.8 %convert_element_type.82 = bf16[64,2048]{1,0:T(8,128)(2,1)} convert(f32[64,2048]{1,0:T(8,128)} %param.5) | non-fusion elementwise | flops 131072 | bytes 786432 | tf_op jit(solution)/shard_map/convert_element_type | solution.py:269
  9.8 1.3 broadcast_in_dim.20.nodes_ref
  11.2 18.3 %shard_map.56 = bf16[2560,1024]{1,0:T(8,128)(2,1)} custom-call(s32[4096]{0:T(1024)S(1)} %bitcast.20, s32[1,1024]{1,0:T(1,128)S(1)} %bitcast.22, s32[8,512,128]{2,1,0:T(8,128)S(1)} %broadcast_in_dim.20.nodes_ref, bf16[8,512,512]{2,1,0:T(8,128)(2,1)} %cell_ref.3), custom_call_target="tpu_custom_call" | custom-call | flops 4294967296 | bytes 9437184 | tf_op jit(solution)/shard_map/pallas_call | solution.py:111
  29.4 10.2 %all-gather.2.cloned.1.call-done = bf16[256,2048]{1,0:T(8,128)(2,1)} async-done(((bf16[64,2048]{1,0:T(8,128)(2,1)}), bf16[256,2048]{1,0:T(8,128)(2,1)}) %all-gather.2.cloned.1.call-update) | async-done | bytes 1048592 | tf_op jit(solution)/shard_map/all_gather | solution.py:269
  39.6 2.4 %fusion.22 = bf16[256,512]{1,0:T(8,128)(2,1)S(1)} fusion(bf16[256,2048]{1,0:T(8,128)(2,1)} %all-gather.2.cloned.1.call-done, s32[512]{0:T(512)S(1)} %pad_add_fusion.1), kind=kOutput, calls=%fused_computation.28 | convolution fusion | flops 538050560 | bytes 1312768 | tf_op jit(solution)/shard_map/dot_general | solution.py:328
  42.7 2.9 %collective-permute-start = (bf16[256,256]{1,0:T(8,128)(2,1)S(1)}, bf16[256,256]{1,0:T(8,128)(2,1)S(1)}, u32[]{:S(2)}, u32[]{:S(2)}) collective-permute-start(bf16[256,256]{1,0:T(8,128)(2,1)S(1)} %get-tuple-element.24), channel_id=1, source_target_pairs={{0,4},{4,0},{8,12},{12,8},{16,20},{20,16},{24,28},{28,24},{1,5},{5... | collective-permute-start | bytes 393224 | tf_op jit(solution)/shard_map/ppermute | solution.py:331
  47.9 2.5 %fusion.75 = (bf16[256,1024]{1,0:T(8,128)(2,1)S(1)}, f32[256,1024]{1,0:T(8,128)}) fusion(bf16[256,2560]{1,0:T(8,128)(2,1)S(1)} %constant_dynamic-update-slice_fusion, bf16[2560,1024]{1,0:T(8,128)(2,1)S(1)} %copy-done.8), kind=kOutput, calls=%fused_computation.105 | convolution fusion | flops 1342439424 | bytes 8126464 | tf_op jit(solution)/shard_map/dot_general | solution.py:309
  51.3 1.5 collective-permute-start.2
  52.8 1.4 collective-permute-start.3
  54.2 33.3 %shard_map.55 = bf16[2560,2048]{1,0:T(8,128)(2,1)} custom-call(s32[4096]{0:T(1024)S(1)} %bitcast.21, s32[1,2048]{1,0:T(1,128)S(1)} %iota_add_fusion.column_ref, s32[8,512,128]{2,1,0:T(8,128)S(1)} %broadcast_in_dim.20.nodes_ref, bf16[8,512,512]{2,1,0:T(8,128)(2,1)} %cell_ref.3), custom_call_target="tpu_custom_call" | custom-call | flops 8589934592 | bytes 18874368 | tf_op jit(solution)/shard_map/pallas_call | solution.py:111
  88.5 1.0 fusion.3
  89.6 6.1 %fusion.76 = (bf16[256,2048]{1,0:T(8,128)(2,1)S(1)}, f32[256,2048]{1,0:T(8,128)S(1)}) fusion(f32[256,2048]{1,0:T(8,128)S(1)} %fusion.3, bf16[256,2560]{1,0:T(8,128)(2,1)S(1)} %copy-done.3, bf16[2560,2048]{1,0:T(8,128)(2,1)} %shard_map.55), kind=kOutput, calls=%fused_computation.106 | convolution fusion | flops 2685403136 | bytes 17039360 | tf_op jit(solution)/shard_map/dot_general | solution.py:309
  95.7 1.7 fusion.58
  97.4 1.5 fusion.77
  99.0 3.6 %collective-permute-start.4 = (bf16[256,512]{1,0:T(8,128)(2,1)S(1)}, bf16[256,512]{1,0:T(8,128)(2,1)S(1)}, u32[]{:S(2)}, u32[]{:S(2)}) collective-permute-start(bf16[256,512]{1,0:T(8,128)(2,1)S(1)} %get-tuple-element.19), channel_id=1, source_target_pairs={{0,4},{4,0},{8,12},{12,8},{16,20},{20,16},{24,28},{28,24},{1,5},{5... | collective-permute-start | bytes 786440 | tf_op jit(solution)/shard_map/ppermute | solution.py:314
  103.7 2.9 %fusion.27 = f32[256,2048]{1,0:T(8,128)S(1)} fusion(bf16[2560,2048]{1,0:T(8,128)(2,1)S(1)} %bitcast.26, bf16[256,256]{1,0:T(8,128)(2,1)S(1)} %get-tuple-element.14, bf16[256,256]{1,0:T(8,128)(2,1)S(1)} %get-tuple-element.13, bf16[256,2048]{1,0:T(8,128)(2,1)S(1)} %get-tuple-element.29), kind=kOutput, calls=%fused_computation.34 | convolution fusion | flops 2688286720 | bytes 13893632 | tf_op jit(solution)/shard_map/dot_general | solution.py:309
  106.8 1.3 fusion.78
  108.1 1.5 fusion.79
  109.7 6.5 %collective-permute-start.6 = (bf16[256,512]{1,0:T(8,128)(2,1)S(1)}, bf16[256,512]{1,0:T(8,128)(2,1)S(1)}, u32[]{:S(2)}, u32[]{:S(2)}) collective-permute-start(bf16[256,512]{1,0:T(8,128)(2,1)S(1)} %get-tuple-element.17), channel_id=1, source_target_pairs={{0,4},{4,0},{8,12},{12,8},{16,20},{20,16},{24,28},{28,24},{1,5},{5... | collective-permute-start | bytes 786440 | tf_op jit(solution)/shard_map/ppermute | solution.py:314
  116.9 2.9 %fusion.25 = f32[256,2048]{1,0:T(8,128)S(1)} fusion(bf16[2560,2048]{1,0:T(8,128)(2,1)S(1)} %bitcast.26, bf16[256,256]{1,0:T(8,128)(2,1)S(1)} %get-tuple-element.12, bf16[256,256]{1,0:T(8,128)(2,1)S(1)} %get-tuple-element.11, bf16[256,2048]{1,0:T(8,128)(2,1)S(1)} %get-tuple-element.33), kind=kOutput, calls=%fused_computation.32 | convolution fusion | flops 2688286720 | bytes 13893632 | tf_op jit(solution)/shard_map/dot_general | solution.py:309
  119.9 1.3 fusion.14
  121.2 1.1 fusion.35
  122.3 1.5 convolution_convert_fusion
  123.9 5.8 %collective-permute-start.8 = (bf16[256,512]{1,0:T(8,128)(2,1)S(1)}, bf16[256,512]{1,0:T(8,128)(2,1)S(1)}, u32[]{:S(2)}, u32[]{:S(2)}) collective-permute-start(bf16[256,512]{1,0:T(8,128)(2,1)S(1)} %get-tuple-element.15), channel_id=1, source_target_pairs={{0,4},{4,0},{8,12},{12,8},{16,20},{20,16},{24,28},{28,24},{1,5},{5... | collective-permute-start | bytes 786440 | tf_op jit(solution)/shard_map/ppermute | solution.py:314
  130.6 2.9 %fusion.23 = f32[256,2048]{1,0:T(8,128)S(1)} fusion(bf16[2560,2048]{1,0:T(8,128)(2,1)S(1)} %bitcast.26, bf16[256,256]{1,0:T(8,128)(2,1)S(1)} %get-tuple-element.10, bf16[256,256]{1,0:T(8,128)(2,1)S(1)} %get-tuple-element.9, bf16[256,2048]{1,0:T(8,128)(2,1)S(1)} %fusion.14), kind=kOutput, calls=%fused_computation.30 | convolution fusion | flops 2688286720 | bytes 13893632 | tf_op jit(solution)/shard_map/dot_general | solution.py:309
  133.6 1.3 fusion.15.filtered_ref
  135.3 6.6 %collective-permute-start.10 = (bf16[256,256]{1,0:T(8,128)(2,1)S(1)}, bf16[256,256]{1,0:T(8,128)(2,1)S(1)}, u32[]{:S(2)}, u32[]{:S(2)}) collective-permute-start(bf16[256,256]{1,0:T(8,128)(2,1)S(1)} %convolution_convert_fusion.1), channel_id=1, source_target_pairs={{0,4},{4,0},{8,12},{12,8},{16,20},{20,16},{24,28},{28,24},{1,5},{5... | collective-permute-start | bytes 393224 | tf_op jit(solution)/shard_map/ppermute | solution.py:255
  143.0 2.6 %collective-permute-start.11 = (bf16[256,256]{1,0:T(8,128)(2,1)S(1)}, bf16[256,256]{1,0:T(8,128)(2,1)S(1)}, u32[]{:S(2)}, u32[]{:S(2)}) collective-permute-start(bf16[256,256]{1,0:T(8,128)(2,1)S(1)} %add_convert_fusion.1), channel_id=1, source_target_pairs={{0,8},{4,12},{8,0},{12,4},{16,24},{20,28},{24,16},{28,20},{1,9},{5... | collective-permute-start | bytes 393224 | tf_op jit(solution)/shard_map/ppermute | solution.py:255
  145.5 4.0 %collective-permute-done.11 = bf16[256,256]{1,0:T(8,128)(2,1)S(1)} collective-permute-done((bf16[256,256]{1,0:T(8,128)(2,1)S(1)}, bf16[256,256]{1,0:T(8,128)(2,1)S(1)}, u32[]{:S(2)}, u32[]{:S(2)}) %collective-permute-start.11) | collective-permute-done | bytes 131104 | tf_op jit(solution)/shard_map/ppermute | solution.py:255
  149.6 2.2 %collective-permute-start.12 = (bf16[256,256]{1,0:T(8,128)(2,1)S(1)}, bf16[256,256]{1,0:T(8,128)(2,1)S(1)}, u32[]{:S(2)}, u32[]{:S(2)}) collective-permute-start(bf16[256,256]{1,0:T(8,128)(2,1)S(1)} %add_convert_fusion), channel_id=1, source_target_pairs={{0,16},{4,20},{8,24},{12,28},{16,0},{20,4},{24,8},{28,12},{1,17},{... | collective-permute-start | bytes 393224 | tf_op jit(solution)/shard_map/ppermute | solution.py:255
  151.7 3.1 %collective-permute-done.12 = bf16[256,256]{1,0:T(8,128)(2,1)S(1)} collective-permute-done((bf16[256,256]{1,0:T(8,128)(2,1)S(1)}, bf16[256,256]{1,0:T(8,128)(2,1)S(1)}, u32[]{:S(2)}, u32[]{:S(2)}) %collective-permute-start.12) | collective-permute-done | bytes 131104 | tf_op jit(solution)/shard_map/ppermute | solution.py:255
  154.9 10.1 %shard_map.57 = f32[64,2048]{1,0:T(8,128)} custom-call(s32[1]{0:T(128)} %bitcast.block_ref, f32[256,256]{1,0:T(8,128)S(1)} %convert_add_fusion.gram_ref, bf16[256,2048]{1,0:T(8,128)(2,1)S(1)} %fusion.15.filtered_ref), custom_call_target="tpu_custom_call" | custom-call | tf_op jit(solution)/shard_map/pallas_call | solution.py:227
  (75 shorter events, 10.8 us)
Async XLA Ops:
  6.5 33.1 %all-gather.2.cloned.1.call-start = ((), (), s32[]{:S(2)}) async-start(), calls=%async_computation | async-start | bytes 1310720 | tf_op jit(solution)/shard_map/all_gather | solution.py:269
  39.6 6.0 %copy-start = (bf16[256,2048]{1,0:T(8,128)(2,1)S(1)}, bf16[256,2048]{1,0:T(8,128)(2,1)}, u32[]{:S(2)}) copy-start(bf16[256,2048]{1,0:T(8,128)(2,1)} %all-gather.2.cloned.1.call-done) | copy-start | bytes 3145732
  39.6 8.3 %copy-start.8 = (bf16[2560,1024]{1,0:T(8,128)(2,1)S(1)}, bf16[2560,1024]{1,0:T(8,128)(2,1)}, u32[]{:S(2)}) copy-start(bf16[2560,1024]{1,0:T(8,128)(2,1)} %shard_map.56) | copy-start | bytes 15728644
  42.1 4.6 %collective-permute-start.1 = (bf16[256,256]{1,0:T(8,128)(2,1)S(1)}, bf16[256,256]{1,0:T(8,128)(2,1)S(1)}, u32[]{:S(2)}, u32[]{:S(2)}) collective-permute-start(bf16[256,256]{1,0:T(8,128)(2,1)S(1)} %get-tuple-element.23), channel_id=1, source_target_pairs={{4,8},{8,4},{12,16},{16,12},{20,24},{24,20},{5,9},{9,5},{13,17},{1... | collective-permute-start | bytes 393224 | tf_op jit(solution)/shard_map/ppermute | solution.py:332
  42.7 3.9 %collective-permute-start = (bf16[256,256]{1,0:T(8,128)(2,1)S(1)}, bf16[256,256]{1,0:T(8,128)(2,1)S(1)}, u32[]{:S(2)}, u32[]{:S(2)}) collective-permute-start(bf16[256,256]{1,0:T(8,128)(2,1)S(1)} %get-tuple-element.24), channel_id=1, source_target_pairs={{0,4},{4,0},{8,12},{12,8},{16,20},{20,16},{24,28},{28,24},{1,5},{5... | collective-permute-start | bytes 393224 | tf_op jit(solution)/shard_map/ppermute | solution.py:331
  46.6 0.6 copy-start.6
  47.3 0.7 copy-start.4
  47.9 2.6 %copy-start.2 = (bf16[256,2560]{1,0:T(8,128)(2,1)}, bf16[256,2560]{1,0:T(8,128)(2,1)S(1)}, u32[]{:S(2)}) copy-start(bf16[256,2560]{1,0:T(8,128)(2,1)S(1)} %constant_dynamic-update-slice_fusion) | copy-start | bytes 3932164
  51.3 36.1 %collective-permute-start.2 = (bf16[256,512]{1,0:T(8,128)(2,1)}, bf16[256,512]{1,0:T(8,128)(2,1)S(1)}, u32[]{:S(2)}, u32[]{:S(2)}) collective-permute-start(bf16[256,512]{1,0:T(8,128)(2,1)} %get-tuple-element.21), channel_id=1, source_target_pairs={{0,4},{4,0},{8,12},{12,8},{16,20},{20,16},{24,28},{28,24},{1,5},{5... | collective-permute-start | bytes 786440 | tf_op jit(solution)/shard_map/ppermute | solution.py:314
  52.8 34.7 %collective-permute-start.3 = (bf16[256,512]{1,0:T(8,128)(2,1)}, bf16[256,512]{1,0:T(8,128)(2,1)}, u32[]{:S(2)}, u32[]{:S(2)}) collective-permute-start(bf16[256,512]{1,0:T(8,128)(2,1)} %get-tuple-element.22), channel_id=1, source_target_pairs={{4,8},{8,4},{12,16},{16,12},{20,24},{24,20},{5,9},{9,5},{13,17},{1... | collective-permute-start | bytes 786440 | tf_op jit(solution)/shard_map/ppermute | solution.py:315
  87.5 2.1 %copy-start.3 = (bf16[256,2560]{1,0:T(8,128)(2,1)S(1)}, bf16[256,2560]{1,0:T(8,128)(2,1)}, u32[]{:S(2)}) copy-start(bf16[256,2560]{1,0:T(8,128)(2,1)} %copy-done.2) | copy-start | bytes 3932164
  88.5 8.9 %slice-start = ((s8[5242880]{0:T(1024)(128)(4,1)}), s8[4194304]{0:T(1024)(128)(4,1)S(1)}, s32[]{:S(2)}) async-start(s8[5242880]{0:T(1024)(128)(4,1)} %bitcast.23), calls=%async_computation.1 | async-start | bytes 8388608
  88.5 15.1 %slice-start.2 = ((s8[10485760]{0:T(1024)(128)(4,1)}), s8[4194304]{0:T(1024)(128)(4,1)S(1)}, s32[]{:S(2)}) async-start(s8[10485760]{0:T(1024)(128)(4,1)} %bitcast.25), calls=%async_computation.3 | async-start | bytes 8388608
  89.6 6.1 %copy-start.1 = (f32[256,1024]{1,0:T(8,128)S(1)}, f32[256,1024]{1,0:T(8,128)}, u32[]{:S(2)}) copy-start(f32[256,1024]{1,0:T(8,128)} %get-tuple-element.28) | copy-start | bytes 3145732
  89.6 7.8 %slice-start.1 = ((s8[5242880]{0:T(1024)(128)(4,1)}), s8[1048576]{0:T(1024)(128)(4,1)S(1)}, s32[]{:S(2)}) async-start(s8[5242880]{0:T(1024)(128)(4,1)} %bitcast.23), calls=%async_computation.2 | async-start | bytes 2097152
  89.6 14.1 %slice-start.3 = ((s8[10485760]{0:T(1024)(128)(4,1)}), s8[4194304]{0:T(1024)(128)(4,1)S(1)}, s32[]{:S(2)}) async-start(s8[10485760]{0:T(1024)(128)(4,1)} %bitcast.25), calls=%async_computation.4 | async-start | bytes 8388608
  89.6 14.1 %slice-start.4 = ((s8[10485760]{0:T(1024)(128)(4,1)}), s8[2097152]{0:T(1024)(128)(4,1)S(1)}, s32[]{:S(2)}) async-start(s8[10485760]{0:T(1024)(128)(4,1)} %bitcast.25), calls=%async_computation.5 | async-start | bytes 4194304
  99.0 7.6 %collective-permute-start.4 = (bf16[256,512]{1,0:T(8,128)(2,1)S(1)}, bf16[256,512]{1,0:T(8,128)(2,1)S(1)}, u32[]{:S(2)}, u32[]{:S(2)}) collective-permute-start(bf16[256,512]{1,0:T(8,128)(2,1)S(1)} %get-tuple-element.19), channel_id=1, source_target_pairs={{0,4},{4,0},{8,12},{12,8},{16,20},{20,16},{24,28},{28,24},{1,5},{5... | collective-permute-start | bytes 786440 | tf_op jit(solution)/shard_map/ppermute | solution.py:314
  102.7 4.0 %copy-start.5 = (bf16[256,256]{1,0:T(8,128)(2,1)S(1)}, bf16[256,256]{1,0:T(8,128)(2,1)}, u32[]{:S(2)}) copy-start(bf16[256,256]{1,0:T(8,128)(2,1)} %copy-done.4) | copy-start | bytes 393220
  102.7 4.0 %copy-start.7 = (bf16[256,256]{1,0:T(8,128)(2,1)S(1)}, bf16[256,256]{1,0:T(8,128)(2,1)}, u32[]{:S(2)}) copy-start(bf16[256,256]{1,0:T(8,128)(2,1)} %copy-done.6) | copy-start | bytes 393220
  102.7 4.0 %collective-permute-start.5 = (bf16[256,512]{1,0:T(8,128)(2,1)S(1)}, bf16[256,512]{1,0:T(8,128)(2,1)S(1)}, u32[]{:S(2)}, u32[]{:S(2)}) collective-permute-start(bf16[256,512]{1,0:T(8,128)(2,1)S(1)} %get-tuple-element.20), channel_id=1, source_target_pairs={{4,8},{8,4},{12,16},{16,12},{20,24},{24,20},{5,9},{9,5},{13,17},{1... | collective-permute-start | bytes 786440 | tf_op jit(solution)/shard_map/ppermute | solution.py:315
  109.7 10.1 %collective-permute-start.6 = (bf16[256,512]{1,0:T(8,128)(2,1)S(1)}, bf16[256,512]{1,0:T(8,128)(2,1)S(1)}, u32[]{:S(2)}, u32[]{:S(2)}) collective-permute-start(bf16[256,512]{1,0:T(8,128)(2,1)S(1)} %get-tuple-element.17), channel_id=1, source_target_pairs={{0,4},{4,0},{8,12},{12,8},{16,20},{20,16},{24,28},{28,24},{1,5},{5... | collective-permute-start | bytes 786440 | tf_op jit(solution)/shard_map/ppermute | solution.py:314
  116.3 3.6 %collective-permute-start.7 = (bf16[256,512]{1,0:T(8,128)(2,1)S(1)}, bf16[256,512]{1,0:T(8,128)(2,1)S(1)}, u32[]{:S(2)}, u32[]{:S(2)}) collective-permute-start(bf16[256,512]{1,0:T(8,128)(2,1)S(1)} %get-tuple-element.18), channel_id=1, source_target_pairs={{4,8},{8,4},{12,16},{16,12},{20,24},{24,20},{5,9},{9,5},{13,17},{1... | collective-permute-start | bytes 786440 | tf_op jit(solution)/shard_map/ppermute | solution.py:315
  123.9 9.6 %collective-permute-start.8 = (bf16[256,512]{1,0:T(8,128)(2,1)S(1)}, bf16[256,512]{1,0:T(8,128)(2,1)S(1)}, u32[]{:S(2)}, u32[]{:S(2)}) collective-permute-start(bf16[256,512]{1,0:T(8,128)(2,1)S(1)} %get-tuple-element.15), channel_id=1, source_target_pairs={{0,4},{4,0},{8,12},{12,8},{16,20},{20,16},{24,28},{28,24},{1,5},{5... | collective-permute-start | bytes 786440 | tf_op jit(solution)/shard_map/ppermute | solution.py:314
  129.7 3.9 %collective-permute-start.9 = (bf16[256,512]{1,0:T(8,128)(2,1)S(1)}, bf16[256,512]{1,0:T(8,128)(2,1)S(1)}, u32[]{:S(2)}, u32[]{:S(2)}) collective-permute-start(bf16[256,512]{1,0:T(8,128)(2,1)S(1)} %get-tuple-element.16), channel_id=1, source_target_pairs={{4,8},{8,4},{12,16},{16,12},{20,24},{24,20},{5,9},{9,5},{13,17},{1... | collective-permute-start | bytes 786440 | tf_op jit(solution)/shard_map/ppermute | solution.py:315
  135.3 7.6 %collective-permute-start.10 = (bf16[256,256]{1,0:T(8,128)(2,1)S(1)}, bf16[256,256]{1,0:T(8,128)(2,1)S(1)}, u32[]{:S(2)}, u32[]{:S(2)}) collective-permute-start(bf16[256,256]{1,0:T(8,128)(2,1)S(1)} %convolution_convert_fusion.1), channel_id=1, source_target_pairs={{0,4},{4,0},{8,12},{12,8},{16,20},{20,16},{24,28},{28,24},{1,5},{5... | collective-permute-start | bytes 393224 | tf_op jit(solution)/shard_map/ppermute | solution.py:255
  143.0 6.6 %collective-permute-start.11 = (bf16[256,256]{1,0:T(8,128)(2,1)S(1)}, bf16[256,256]{1,0:T(8,128)(2,1)S(1)}, u32[]{:S(2)}, u32[]{:S(2)}) collective-permute-start(bf16[256,256]{1,0:T(8,128)(2,1)S(1)} %add_convert_fusion.1), channel_id=1, source_target_pairs={{0,8},{4,12},{8,0},{12,4},{16,24},{20,28},{24,16},{28,20},{1,9},{5... | collective-permute-start | bytes 393224 | tf_op jit(solution)/shard_map/ppermute | solution.py:255
  149.6 5.3 %collective-permute-start.12 = (bf16[256,256]{1,0:T(8,128)(2,1)S(1)}, bf16[256,256]{1,0:T(8,128)(2,1)S(1)}, u32[]{:S(2)}, u32[]{:S(2)}) collective-permute-start(bf16[256,256]{1,0:T(8,128)(2,1)S(1)} %add_convert_fusion), channel_id=1, source_target_pairs={{0,16},{4,20},{8,24},{12,28},{16,0},{20,4},{24,8},{28,12},{1,17},{... | collective-permute-start | bytes 393224 | tf_op jit(solution)/shard_map/ppermute | solution.py:255
Sparse Core Ops, SparseCore 0:
  8.9 30.6 all-gather.1

commit v2 on v1

--- a/solution.py
+++ b/solution.py
@@ -12,7 +12,22 @@
 LANES = 128
 SUBLANES = 8
 CHUNK = LANES * SUBLANES
-PITCH = SUBLANES + 1
+
+
+def turn(tiles):
+    row = lax.broadcasted_iota(jnp.int32, (SUBLANES, LANES), 0)
+    tiles = [pltpu.roll(tile, i, 0) if i else tile for i, tile in enumerate(tiles)]
+    step = 1
+    while step < SUBLANES:
+        far = (row & step) != 0
+        tiles = [
+            jnp.where(far, tiles[(i + step) % SUBLANES], tiles[i]) for i in range(SUBLANES)
+        ]
+        step *= 2
+    tiles = [tiles[-i % SUBLANES] for i in range(SUBLANES)]
+    return [
+        pltpu.roll(tile, SUBLANES - i, 0) if i else tile for i, tile in enumerate(tiles)
+    ]
 
 
 def assemble_kernel(places_ref, column_ref, nodes_ref, cell_ref, out_ref, total, even_terms, odd_terms):
@@ -38,21 +53,22 @@
         return jnp.dot(cell_ref[0], picker, preferred_element_type=jnp.float32)
 
     def keep_part(part, spread, terms):
-        for first in range(0, cell_nodes, SUBLANES):
-            for half in range(2):
-                terms[pl.ds(first * PITCH + 2 * part + half, SUBLANES, stride=PITCH), :] = spread[
-                    first : first + SUBLANES, half * LANES : (half + 1) * LANES
-                ]
+        for half in range(2):
+            terms[2 * part + half] = spread[:, half * LANES : (half + 1) * LANES]
 
     def add_part(part, of_cell, terms):
-        first = part * part_rows
+        first = pl.multiple_of(part * part_rows, part_rows)
         for start in range(0, part_rows, group):
-            places = [places_ref[of_cell * cell_nodes + first + start + k] for k in range(group)]
-            sums = [
-                total[pl.ds(places[k], SUBLANES), :]
-                + terms[pl.ds((first + start + k) * PITCH, SUBLANES), :]
+            places = [
+                pl.multiple_of(places_ref[of_cell * cell_nodes + first + start + k], SUBLANES)
                 for k in range(group)
             ]
+            added = []
+            for inner in range(0, group, SUBLANES):
+                added += turn(
+                    [terms[b, pl.ds(first + start + inner, SUBLANES), :] for b in range(SUBLANES)]
+                )
+            sums = [total[pl.ds(places[k], SUBLANES), :] + added[k] for k in range(group)]
             for k in range(group):
                 total[pl.ds(places[k], SUBLANES), :] = sums[k]
 
@@ -94,11 +110,18 @@
     def _():
         def write_rows(step, carry):
             first = pl.multiple_of(step * 16, 16)
+            upper, lower = (
+                turn(
+                    [
+                        total[pl.ds(pl.multiple_of((first + start + i) * SUBLANES, SUBLANES), SUBLANES), :]
+                        for i in range(SUBLANES)
+                    ]
+                )
+                for start in (0, SUBLANES)
+            )
             for block in range(SUBLANES):
-                upper = total[pl.ds(first * PITCH + block, SUBLANES, stride=PITCH), :]
-                lower = total[pl.ds((first + 8) * PITCH + block, SUBLANES, stride=PITCH), :]
                 out_ref[pl.ds(first, 16), block * LANES : (block + 1) * LANES] = jnp.concatenate(
-                    [upper, lower], axis=0
+                    [upper[block], lower[block]], axis=0
                 ).astype(jnp.bfloat16)
             return carry
 
@@ -121,9 +144,9 @@
             ],
             out_specs=pl.BlockSpec((ext_count, CHUNK), lambda q, c, places: (0, q)),
             scratch_shapes=[
-                pltpu.VMEM((ext_count * PITCH, LANES), jnp.float32),
-                pltpu.VMEM((cell_nodes * PITCH, LANES), jnp.float32),
-                pltpu.VMEM((cell_nodes * PITCH, LANES), jnp.float32),
+                pltpu.VMEM((ext_count * SUBLANES, LANES), jnp.float32),
+                pltpu.VMEM((SUBLANES, cell_nodes, LANES), jnp.float32),
+                pltpu.VMEM((SUBLANES, cell_nodes, LANES), jnp.float32),
             ],
         ),
         compiler_params=pltpu.CompilerParams(vmem_limit_bytes=48 * 1024 * 1024),
@@ -289,7 +312,7 @@
             connectivity - face,
             connectivity - (face + own_count) + upper_at,
         ),
-    ).reshape(-1) * PITCH
+    ).reshape(-1) * SUBLANES
     shared_columns = jnp.concatenate([ghost_a, face_a + face, ghost_b, face_b + face])
     own_columns = jnp.arange(own_count, dtype=jnp.int32) + face
 

time: 172 us -> 176 us (1.023)
  Pallas kernels: 61.6 us -> 66.6 us
    pallas_call x2, Pallas kernels: 51.5 us -> 56.5 us  [assemble(): pl.pallas_call(assemble_kernel, out_shape=jax.ShapeDtypeStruct((ext_count...]
  transfers between devices with their start and end apart: 14 -> 14, of which waited for: 5 -> 5; matrix products, arithmetic and copies ran while one was open for 7% -> 7% of each run, Pallas kernels for 30% -> 32%
where the time goes in v2:
time: 176 us; the launch traced here: 175 us
  Pallas kernels  66.6 us (38%)
  starting transfers between devices  36.3 us (21%)
  matrix products  29.8 us (17%)
  waiting for transfers between devices  17.6 us (10%)
  between operations  13.9 us (8%)
  other arithmetic  6.25 us (4%)
  local copies, waits for them, and re-layouts  4.8 us (3%)
    pallas_call x2, Pallas kernels, assemble(): pl.pallas_call(assemble_kernel, out_shape=jax.ShapeDtypeStruct((ext_count...  56.5 us
    dot_general x12, matrix products, times(): return jnp.dot(left, right, preferred_element_type=jnp.float32)  26.9 us
    ppermute x4, starting transfers between devices, apply_hamiltonian(): got_a = lax.ppermute(sent[:, :2 * face], 'slab', pairs_a)  17.6 us
    ppermute x3, starting transfers between devices, sum_over(): got = lax.ppermute(sent, axis, [(i, i ^ step) for i in range(count)])  11.2 us
    pallas_call x1, Pallas kernels, orthonormal(): pl.pallas_call(functools.partial(orthonormal_kernel, scale), out_shape=ja...  10.1 us
    all_gather x1, waiting for transfers between devices, per_device(): lax.all_gather(orbitals.astype(jnp.bfloat16), 'orb', axis=0, tiled=True)  8.49 us
    ppermute x3, waiting for transfers between devices, sum_over(): got = lax.ppermute(sent, axis, [(i, i ^ step) for i in range(count)])  8.14 us
    ppermute x4, starting transfers between devices, apply_hamiltonian(): got_b = lax.ppermute(sent[:, 2 * face:], 'slab', pairs_b)  3.91 us
  transfers between devices with their start and end apart: 14, of which 5 were waited for; matrix products, arithmetic and copies ran while one was open for 7% of the time, Pallas kernels for 32%

profile of v2, /device:TPU:0, one launch (start us, length us, event | category | flops | bytes accessed | tf_op | source)
XLA Modules:
  0.0 175.2 jit_solution(11269862332346850491)
XLA Ops:
  6.5 1.8 %convert_element_type.82 = bf16[64,2048]{1,0:T(8,128)(2,1)} convert(f32[64,2048]{1,0:T(8,128)} %param.5) | non-fusion elementwise | flops 131072 | bytes 786432 | tf_op jit(solution)/shard_map/convert_element_type | solution.py:292
  9.8 1.3 broadcast_in_dim.20.nodes_ref
  11.2 19.9 %shard_map.56 = bf16[2560,1024]{1,0:T(8,128)(2,1)} custom-call(s32[4096]{0:T(1024)S(1)} %bitcast.20, s32[1,1024]{1,0:T(1,128)S(1)} %bitcast.22, s32[8,512,128]{2,1,0:T(8,128)S(1)} %broadcast_in_dim.20.nodes_ref, bf16[8,512,512]{2,1,0:T(8,128)(2,1)} %cell_ref.3), custom_call_target="tpu_custom_call" | custom-call | flops 4294967296 | bytes 9437184 | tf_op jit(solution)/shard_map/pallas_call | solution.py:134
  31.1 8.5 %all-gather.2.cloned.1.call-done = bf16[256,2048]{1,0:T(8,128)(2,1)} async-done(((bf16[64,2048]{1,0:T(8,128)(2,1)}), bf16[256,2048]{1,0:T(8,128)(2,1)}) %all-gather.2.cloned.1.call-update) | async-done | bytes 1048592 | tf_op jit(solution)/shard_map/all_gather | solution.py:292
  39.6 2.4 %fusion.22 = bf16[256,512]{1,0:T(8,128)(2,1)S(1)} fusion(bf16[256,2048]{1,0:T(8,128)(2,1)} %all-gather.2.cloned.1.call-done, s32[512]{0:T(512)S(1)} %pad_add_fusion.1), kind=kOutput, calls=%fused_computation.28 | convolution fusion | flops 538050560 | bytes 1312768 | tf_op jit(solution)/shard_map/dot_general | solution.py:351
  42.7 2.9 %collective-permute-start = (bf16[256,256]{1,0:T(8,128)(2,1)S(1)}, bf16[256,256]{1,0:T(8,128)(2,1)S(1)}, u32[]{:S(2)}, u32[]{:S(2)}) collective-permute-start(bf16[256,256]{1,0:T(8,128)(2,1)S(1)} %get-tuple-element.24), channel_id=1, source_target_pairs={{0,4},{4,0},{8,12},{12,8},{16,20},{20,16},{24,28},{28,24},{1,5},{5... | collective-permute-start | bytes 393224 | tf_op jit(solution)/shard_map/ppermute | solution.py:354
  48.0 2.5 %fusion.75 = (bf16[256,1024]{1,0:T(8,128)(2,1)S(1)}, f32[256,1024]{1,0:T(8,128)}) fusion(bf16[256,2560]{1,0:T(8,128)(2,1)S(1)} %constant_dynamic-update-slice_fusion, bf16[2560,1024]{1,0:T(8,128)(2,1)S(1)} %copy-done.8), kind=kOutput, calls=%fused_computation.105 | convolution fusion | flops 1342439424 | bytes 8126464 | tf_op jit(solution)/shard_map/dot_general | solution.py:332
  51.3 1.5 collective-permute-start.2
  52.8 1.4 collective-permute-start.3
  54.2 36.6 %shard_map.55 = bf16[2560,2048]{1,0:T(8,128)(2,1)} custom-call(s32[4096]{0:T(1024)S(1)} %bitcast.21, s32[1,2048]{1,0:T(1,128)S(1)} %iota_add_fusion.column_ref, s32[8,512,128]{2,1,0:T(8,128)S(1)} %broadcast_in_dim.20.nodes_ref, bf16[8,512,512]{2,1,0:T(8,128)(2,1)} %cell_ref.3), custom_call_target="tpu_custom_call" | custom-call | flops 8589934592 | bytes 18874368 | tf_op jit(solution)/shard_map/pallas_call | solution.py:134
  91.8 1.0 fusion.3
  92.9 6.1 %fusion.76 = (bf16[256,2048]{1,0:T(8,128)(2,1)S(1)}, f32[256,2048]{1,0:T(8,128)S(1)}) fusion(f32[256,2048]{1,0:T(8,128)S(1)} %fusion.3, bf16[256,2560]{1,0:T(8,128)(2,1)S(1)} %copy-done.3, bf16[2560,2048]{1,0:T(8,128)(2,1)} %shard_map.55), kind=kOutput, calls=%fused_computation.106 | convolution fusion | flops 2685403136 | bytes 17039360 | tf_op jit(solution)/shard_map/dot_general | solution.py:332
  99.0 1.7 fusion.58
  100.7 1.5 fusion.77
  102.3 3.7 %collective-permute-start.4 = (bf16[256,512]{1,0:T(8,128)(2,1)S(1)}, bf16[256,512]{1,0:T(8,128)(2,1)S(1)}, u32[]{:S(2)}, u32[]{:S(2)}) collective-permute-start(bf16[256,512]{1,0:T(8,128)(2,1)S(1)} %get-tuple-element.19), channel_id=1, source_target_pairs={{0,4},{4,0},{8,12},{12,8},{16,20},{20,16},{24,28},{28,24},{1,5},{5... | collective-permute-start | bytes 786440 | tf_op jit(solution)/shard_map/ppermute | solution.py:337
  107.1 2.9 %fusion.27 = f32[256,2048]{1,0:T(8,128)S(1)} fusion(bf16[2560,2048]{1,0:T(8,128)(2,1)S(1)} %bitcast.26, bf16[256,256]{1,0:T(8,128)(2,1)S(1)} %get-tuple-element.14, bf16[256,256]{1,0:T(8,128)(2,1)S(1)} %get-tuple-element.13, bf16[256,2048]{1,0:T(8,128)(2,1)S(1)} %get-tuple-element.29), kind=kOutput, calls=%fused_computation.34 | convolution fusion | flops 2688286720 | bytes 13893632 | tf_op jit(solution)/shard_map/dot_general | solution.py:332
  110.2 1.3 fusion.78
  111.5 1.5 fusion.79
  113.1 6.6 %collective-permute-start.6 = (bf16[256,512]{1,0:T(8,128)(2,1)S(1)}, bf16[256,512]{1,0:T(8,128)(2,1)S(1)}, u32[]{:S(2)}, u32[]{:S(2)}) collective-permute-start(bf16[256,512]{1,0:T(8,128)(2,1)S(1)} %get-tuple-element.17), channel_id=1, source_target_pairs={{0,4},{4,0},{8,12},{12,8},{16,20},{20,16},{24,28},{28,24},{1,5},{5... | collective-permute-start | bytes 786440 | tf_op jit(solution)/shard_map/ppermute | solution.py:337
  120.4 2.9 %fusion.25 = f32[256,2048]{1,0:T(8,128)S(1)} fusion(bf16[2560,2048]{1,0:T(8,128)(2,1)S(1)} %bitcast.26, bf16[256,256]{1,0:T(8,128)(2,1)S(1)} %get-tuple-element.12, bf16[256,256]{1,0:T(8,128)(2,1)S(1)} %get-tuple-element.11, bf16[256,2048]{1,0:T(8,128)(2,1)S(1)} %get-tuple-element.33), kind=kOutput, calls=%fused_computation.32 | convolution fusion | flops 2688286720 | bytes 13893632 | tf_op jit(solution)/shard_map/dot_general | solution.py:332
  123.4 1.3 fusion.14
  124.6 1.1 fusion.35
  125.7 1.5 convolution_convert_fusion
  127.3 5.9 %collective-permute-start.8 = (bf16[256,512]{1,0:T(8,128)(2,1)S(1)}, bf16[256,512]{1,0:T(8,128)(2,1)S(1)}, u32[]{:S(2)}, u32[]{:S(2)}) collective-permute-start(bf16[256,512]{1,0:T(8,128)(2,1)S(1)} %get-tuple-element.15), channel_id=1, source_target_pairs={{0,4},{4,0},{8,12},{12,8},{16,20},{20,16},{24,28},{28,24},{1,5},{5... | collective-permute-start | bytes 786440 | tf_op jit(solution)/shard_map/ppermute | solution.py:337
  134.1 2.9 %fusion.23 = f32[256,2048]{1,0:T(8,128)S(1)} fusion(bf16[2560,2048]{1,0:T(8,128)(2,1)S(1)} %bitcast.26, bf16[256,256]{1,0:T(8,128)(2,1)S(1)} %get-tuple-element.10, bf16[256,256]{1,0:T(8,128)(2,1)S(1)} %get-tuple-element.9, bf16[256,2048]{1,0:T(8,128)(2,1)S(1)} %fusion.14), kind=kOutput, calls=%fused_computation.30 | convolution fusion | flops 2688286720 | bytes 13893632 | tf_op jit(solution)/shard_map/dot_general | solution.py:332
  137.1 1.3 fusion.15.filtered_ref
  138.8 6.5 %collective-permute-start.10 = (bf16[256,256]{1,0:T(8,128)(2,1)S(1)}, bf16[256,256]{1,0:T(8,128)(2,1)S(1)}, u32[]{:S(2)}, u32[]{:S(2)}) collective-permute-start(bf16[256,256]{1,0:T(8,128)(2,1)S(1)} %convolution_convert_fusion.1), channel_id=1, source_target_pairs={{0,4},{4,0},{8,12},{12,8},{16,20},{20,16},{24,28},{28,24},{1,5},{5... | collective-permute-start | bytes 393224 | tf_op jit(solution)/shard_map/ppermute | solution.py:278
  146.3 2.7 %collective-permute-start.11 = (bf16[256,256]{1,0:T(8,128)(2,1)S(1)}, bf16[256,256]{1,0:T(8,128)(2,1)S(1)}, u32[]{:S(2)}, u32[]{:S(2)}) collective-permute-start(bf16[256,256]{1,0:T(8,128)(2,1)S(1)} %add_convert_fusion.1), channel_id=1, source_target_pairs={{0,8},{4,12},{8,0},{12,4},{16,24},{20,28},{24,16},{28,20},{1,9},{5... | collective-permute-start | bytes 393224 | tf_op jit(solution)/shard_map/ppermute | solution.py:278
  149.0 4.0 %collective-permute-done.11 = bf16[256,256]{1,0:T(8,128)(2,1)S(1)} collective-permute-done((bf16[256,256]{1,0:T(8,128)(2,1)S(1)}, bf16[256,256]{1,0:T(8,128)(2,1)S(1)}, u32[]{:S(2)}, u32[]{:S(2)}) %collective-permute-start.11) | collective-permute-done | bytes 131104 | tf_op jit(solution)/shard_map/ppermute | solution.py:278
  153.0 2.1 %collective-permute-start.12 = (bf16[256,256]{1,0:T(8,128)(2,1)S(1)}, bf16[256,256]{1,0:T(8,128)(2,1)S(1)}, u32[]{:S(2)}, u32[]{:S(2)}) collective-permute-start(bf16[256,256]{1,0:T(8,128)(2,1)S(1)} %add_convert_fusion), channel_id=1, source_target_pairs={{0,16},{4,20},{8,24},{12,28},{16,0},{20,4},{24,8},{28,12},{1,17},{... | collective-permute-start | bytes 393224 | tf_op jit(solution)/shard_map/ppermute | solution.py:278
  155.1 3.1 %collective-permute-done.12 = bf16[256,256]{1,0:T(8,128)(2,1)S(1)} collective-permute-done((bf16[256,256]{1,0:T(8,128)(2,1)S(1)}, bf16[256,256]{1,0:T(8,128)(2,1)S(1)}, u32[]{:S(2)}, u32[]{:S(2)}) %collective-permute-start.12) | collective-permute-done | bytes 131104 | tf_op jit(solution)/shard_map/ppermute | solution.py:278
  158.3 10.1 %shard_map.57 = f32[64,2048]{1,0:T(8,128)} custom-call(s32[1]{0:T(128)} %bitcast.block_ref, f32[256,256]{1,0:T(8,128)S(1)} %convert_add_fusion.gram_ref, bf16[256,2048]{1,0:T(8,128)(2,1)S(1)} %fusion.15.filtered_ref), custom_call_target="tpu_custom_call" | custom-call | tf_op jit(solution)/shard_map/pallas_call | solution.py:250
  (75 shorter events, 10.8 us)
Async XLA Ops:
  6.5 33.1 %all-gather.2.cloned.1.call-start = ((), (), s32[]{:S(2)}) async-start(), calls=%async_computation | async-start | bytes 1310720 | tf_op jit(solution)/shard_map/all_gather | solution.py:292
  39.6 6.0 %copy-start = (bf16[256,2048]{1,0:T(8,128)(2,1)S(1)}, bf16[256,2048]{1,0:T(8,128)(2,1)}, u32[]{:S(2)}) copy-start(bf16[256,2048]{1,0:T(8,128)(2,1)} %all-gather.2.cloned.1.call-done) | copy-start | bytes 3145732
  39.6 8.3 %copy-start.8 = (bf16[2560,1024]{1,0:T(8,128)(2,1)S(1)}, bf16[2560,1024]{1,0:T(8,128)(2,1)}, u32[]{:S(2)}) copy-start(bf16[2560,1024]{1,0:T(8,128)(2,1)} %shard_map.56) | copy-start | bytes 15728644
  42.1 4.6 %collective-permute-start.1 = (bf16[256,256]{1,0:T(8,128)(2,1)S(1)}, bf16[256,256]{1,0:T(8,128)(2,1)S(1)}, u32[]{:S(2)}, u32[]{:S(2)}) collective-permute-start(bf16[256,256]{1,0:T(8,128)(2,1)S(1)} %get-tuple-element.23), channel_id=1, source_target_pairs={{4,8},{8,4},{12,16},{16,12},{20,24},{24,20},{5,9},{9,5},{13,17},{1... | collective-permute-start | bytes 393224 | tf_op jit(solution)/shard_map/ppermute | solution.py:355
  42.7 3.9 %collective-permute-start = (bf16[256,256]{1,0:T(8,128)(2,1)S(1)}, bf16[256,256]{1,0:T(8,128)(2,1)S(1)}, u32[]{:S(2)}, u32[]{:S(2)}) collective-permute-start(bf16[256,256]{1,0:T(8,128)(2,1)S(1)} %get-tuple-element.24), channel_id=1, source_target_pairs={{0,4},{4,0},{8,12},{12,8},{16,20},{20,16},{24,28},{28,24},{1,5},{5... | collective-permute-start | bytes 393224 | tf_op jit(solution)/shard_map/ppermute | solution.py:354
  46.6 0.6 copy-start.6
  47.3 0.7 copy-start.4
  47.9 2.6 %copy-start.2 = (bf16[256,2560]{1,0:T(8,128)(2,1)}, bf16[256,2560]{1,0:T(8,128)(2,1)S(1)}, u32[]{:S(2)}) copy-start(bf16[256,2560]{1,0:T(8,128)(2,1)S(1)} %constant_dynamic-update-slice_fusion) | copy-start | bytes 3932164
  51.3 39.4 %collective-permute-start.2 = (bf16[256,512]{1,0:T(8,128)(2,1)}, bf16[256,512]{1,0:T(8,128)(2,1)S(1)}, u32[]{:S(2)}, u32[]{:S(2)}) collective-permute-start(bf16[256,512]{1,0:T(8,128)(2,1)} %get-tuple-element.21), channel_id=1, source_target_pairs={{0,4},{4,0},{8,12},{12,8},{16,20},{20,16},{24,28},{28,24},{1,5},{5... | collective-permute-start | bytes 786440 | tf_op jit(solution)/shard_map/ppermute | solution.py:337
  52.8 38.0 %collective-permute-start.3 = (bf16[256,512]{1,0:T(8,128)(2,1)}, bf16[256,512]{1,0:T(8,128)(2,1)}, u32[]{:S(2)}, u32[]{:S(2)}) collective-permute-start(bf16[256,512]{1,0:T(8,128)(2,1)} %get-tuple-element.22), channel_id=1, source_target_pairs={{4,8},{8,4},{12,16},{16,12},{20,24},{24,20},{5,9},{9,5},{13,17},{1... | collective-permute-start | bytes 786440 | tf_op jit(solution)/shard_map/ppermute | solution.py:338
  90.8 2.1 %copy-start.3 = (bf16[256,2560]{1,0:T(8,128)(2,1)S(1)}, bf16[256,2560]{1,0:T(8,128)(2,1)}, u32[]{:S(2)}) copy-start(bf16[256,2560]{1,0:T(8,128)(2,1)} %copy-done.2) | copy-start | bytes 3932164
  91.8 8.9 %slice-start = ((s8[5242880]{0:T(1024)(128)(4,1)}), s8[4194304]{0:T(1024)(128)(4,1)S(1)}, s32[]{:S(2)}) async-start(s8[5242880]{0:T(1024)(128)(4,1)} %bitcast.23), calls=%async_computation.1 | async-start | bytes 8388608
  91.8 15.2 %slice-start.2 = ((s8[10485760]{0:T(1024)(128)(4,1)}), s8[4194304]{0:T(1024)(128)(4,1)S(1)}, s32[]{:S(2)}) async-start(s8[10485760]{0:T(1024)(128)(4,1)} %bitcast.25), calls=%async_computation.3 | async-start | bytes 8388608
  92.9 6.1 %copy-start.1 = (f32[256,1024]{1,0:T(8,128)S(1)}, f32[256,1024]{1,0:T(8,128)}, u32[]{:S(2)}) copy-start(f32[256,1024]{1,0:T(8,128)} %get-tuple-element.28) | copy-start | bytes 3145732
  92.9 7.8 %slice-start.1 = ((s8[5242880]{0:T(1024)(128)(4,1)}), s8[1048576]{0:T(1024)(128)(4,1)S(1)}, s32[]{:S(2)}) async-start(s8[5242880]{0:T(1024)(128)(4,1)} %bitcast.23), calls=%async_computation.2 | async-start | bytes 2097152
  92.9 14.1 %slice-start.3 = ((s8[10485760]{0:T(1024)(128)(4,1)}), s8[4194304]{0:T(1024)(128)(4,1)S(1)}, s32[]{:S(2)}) async-start(s8[10485760]{0:T(1024)(128)(4,1)} %bitcast.25), calls=%async_computation.4 | async-start | bytes 8388608
  92.9 14.1 %slice-start.4 = ((s8[10485760]{0:T(1024)(128)(4,1)}), s8[2097152]{0:T(1024)(128)(4,1)S(1)}, s32[]{:S(2)}) async-start(s8[10485760]{0:T(1024)(128)(4,1)} %bitcast.25), calls=%async_computation.5 | async-start | bytes 4194304
  102.3 7.7 %collective-permute-start.4 = (bf16[256,512]{1,0:T(8,128)(2,1)S(1)}, bf16[256,512]{1,0:T(8,128)(2,1)S(1)}, u32[]{:S(2)}, u32[]{:S(2)}) collective-permute-start(bf16[256,512]{1,0:T(8,128)(2,1)S(1)} %get-tuple-element.19), channel_id=1, source_target_pairs={{0,4},{4,0},{8,12},{12,8},{16,20},{20,16},{24,28},{28,24},{1,5},{5... | collective-permute-start | bytes 786440 | tf_op jit(solution)/shard_map/ppermute | solution.py:337
  106.1 4.0 %copy-start.5 = (bf16[256,256]{1,0:T(8,128)(2,1)S(1)}, bf16[256,256]{1,0:T(8,128)(2,1)}, u32[]{:S(2)}) copy-start(bf16[256,256]{1,0:T(8,128)(2,1)} %copy-done.4) | copy-start | bytes 393220
  106.1 4.0 %copy-start.7 = (bf16[256,256]{1,0:T(8,128)(2,1)S(1)}, bf16[256,256]{1,0:T(8,128)(2,1)}, u32[]{:S(2)}) copy-start(bf16[256,256]{1,0:T(8,128)(2,1)} %copy-done.6) | copy-start | bytes 393220
  106.1 4.0 %collective-permute-start.5 = (bf16[256,512]{1,0:T(8,128)(2,1)S(1)}, bf16[256,512]{1,0:T(8,128)(2,1)S(1)}, u32[]{:S(2)}, u32[]{:S(2)}) collective-permute-start(bf16[256,512]{1,0:T(8,128)(2,1)S(1)} %get-tuple-element.20), channel_id=1, source_target_pairs={{4,8},{8,4},{12,16},{16,12},{20,24},{24,20},{5,9},{9,5},{13,17},{1... | collective-permute-start | bytes 786440 | tf_op jit(solution)/shard_map/ppermute | solution.py:338
  113.1 10.2 %collective-permute-start.6 = (bf16[256,512]{1,0:T(8,128)(2,1)S(1)}, bf16[256,512]{1,0:T(8,128)(2,1)S(1)}, u32[]{:S(2)}, u32[]{:S(2)}) collective-permute-start(bf16[256,512]{1,0:T(8,128)(2,1)S(1)} %get-tuple-element.17), channel_id=1, source_target_pairs={{0,4},{4,0},{8,12},{12,8},{16,20},{20,16},{24,28},{28,24},{1,5},{5... | collective-permute-start | bytes 786440 | tf_op jit(solution)/shard_map/ppermute | solution.py:337
  119.7 3.6 %collective-permute-start.7 = (bf16[256,512]{1,0:T(8,128)(2,1)S(1)}, bf16[256,512]{1,0:T(8,128)(2,1)S(1)}, u32[]{:S(2)}, u32[]{:S(2)}) collective-permute-start(bf16[256,512]{1,0:T(8,128)(2,1)S(1)} %get-tuple-element.18), channel_id=1, source_target_pairs={{4,8},{8,4},{12,16},{16,12},{20,24},{24,20},{5,9},{9,5},{13,17},{1... | collective-permute-start | bytes 786440 | tf_op jit(solution)/shard_map/ppermute | solution.py:338
  127.3 9.7 %collective-permute-start.8 = (bf16[256,512]{1,0:T(8,128)(2,1)S(1)}, bf16[256,512]{1,0:T(8,128)(2,1)S(1)}, u32[]{:S(2)}, u32[]{:S(2)}) collective-permute-start(bf16[256,512]{1,0:T(8,128)(2,1)S(1)} %get-tuple-element.15), channel_id=1, source_target_pairs={{0,4},{4,0},{8,12},{12,8},{16,20},{20,16},{24,28},{28,24},{1,5},{5... | collective-permute-start | bytes 786440 | tf_op jit(solution)/shard_map/ppermute | solution.py:337
  133.2 3.9 %collective-permute-start.9 = (bf16[256,512]{1,0:T(8,128)(2,1)S(1)}, bf16[256,512]{1,0:T(8,128)(2,1)S(1)}, u32[]{:S(2)}, u32[]{:S(2)}) collective-permute-start(bf16[256,512]{1,0:T(8,128)(2,1)S(1)} %get-tuple-element.16), channel_id=1, source_target_pairs={{4,8},{8,4},{12,16},{16,12},{20,24},{24,20},{5,9},{9,5},{13,17},{1... | collective-permute-start | bytes 786440 | tf_op jit(solution)/shard_map/ppermute | solution.py:338
  138.8 7.4 %collective-permute-start.10 = (bf16[256,256]{1,0:T(8,128)(2,1)S(1)}, bf16[256,256]{1,0:T(8,128)(2,1)S(1)}, u32[]{:S(2)}, u32[]{:S(2)}) collective-permute-start(bf16[256,256]{1,0:T(8,128)(2,1)S(1)} %convolution_convert_fusion.1), channel_id=1, source_target_pairs={{0,4},{4,0},{8,12},{12,8},{16,20},{20,16},{24,28},{28,24},{1,5},{5... | collective-permute-start | bytes 393224 | tf_op jit(solution)/shard_map/ppermute | solution.py:278
  146.3 6.7 %collective-permute-start.11 = (bf16[256,256]{1,0:T(8,128)(2,1)S(1)}, bf16[256,256]{1,0:T(8,128)(2,1)S(1)}, u32[]{:S(2)}, u32[]{:S(2)}) collective-permute-start(bf16[256,256]{1,0:T(8,128)(2,1)S(1)} %add_convert_fusion.1), channel_id=1, source_target_pairs={{0,8},{4,12},{8,0},{12,4},{16,24},{20,28},{24,16},{28,20},{1,9},{5... | collective-permute-start | bytes 393224 | tf_op jit(solution)/shard_map/ppermute | solution.py:278
  153.0 5.3 %collective-permute-start.12 = (bf16[256,256]{1,0:T(8,128)(2,1)S(1)}, bf16[256,256]{1,0:T(8,128)(2,1)S(1)}, u32[]{:S(2)}, u32[]{:S(2)}) collective-permute-start(bf16[256,256]{1,0:T(8,128)(2,1)S(1)} %add_convert_fusion), channel_id=1, source_target_pairs={{0,16},{4,20},{8,24},{12,28},{16,0},{20,4},{24,8},{28,12},{1,17},{... | collective-permute-start | bytes 393224 | tf_op jit(solution)/shard_map/ppermute | solution.py:278
Sparse Core Ops, SparseCore 0:
  8.9 30.6 all-gather.1

commit v3 on v1

--- a/solution.py
+++ b/solution.py
@@ -15,11 +15,14 @@
 PITCH = SUBLANES + 1
 
 
-def assemble_kernel(places_ref, column_ref, nodes_ref, cell_ref, out_ref, total, even_terms, odd_terms):
+def assemble_kernel(
+    places_ref, column_ref, nodes_ref, cell_ref, shared_ref, own_ref, total, even_terms, odd_terms
+):
+    chunk = pl.program_id(0)
     cell = pl.program_id(1)
     cells = pl.num_programs(1)
     cell_nodes = cell_ref.shape[1]
-    ext_count = out_ref.shape[0]
+    ext_count = shared_ref.shape[0]
     parts = CHUNK // 256
     part_rows = cell_nodes // parts
     group = 32
@@ -90,8 +93,7 @@
 
             lax.fori_loop(0, parts, body, 0)
 
-    @pl.when(cell == cells - 1)
-    def _():
+    def write_out(out_ref):
         def write_rows(step, carry):
             first = pl.multiple_of(step * 16, 16)
             for block in range(SUBLANES):
@@ -104,13 +106,24 @@
 
         lax.fori_loop(0, ext_count // 16, write_rows, 0, unroll=4)
 
+    @pl.when((cell == cells - 1) & (chunk == 0))
+    def _():
+        write_out(shared_ref)
+
+    @pl.when((cell == cells - 1) & (chunk > 0))
+    def _():
+        write_out(own_ref)
+
 
 def assemble(places, columns, nodes, cell_matrices, ext_count):
     cells, cell_nodes, _ = cell_matrices.shape
     chunks = columns.shape[0] // CHUNK
     return pl.pallas_call(
         assemble_kernel,
-        out_shape=jax.ShapeDtypeStruct((ext_count, columns.shape[0]), jnp.bfloat16),
+        out_shape=(
+            jax.ShapeDtypeStruct((ext_count, CHUNK), jnp.bfloat16),
+            jax.ShapeDtypeStruct((ext_count, columns.shape[0] - CHUNK), jnp.bfloat16),
+        ),
         grid_spec=pltpu.PrefetchScalarGridSpec(
             num_scalar_prefetch=1,
             grid=(chunks, cells),
@@ -119,7 +132,10 @@
                 pl.BlockSpec((1, cell_nodes, LANES), lambda q, c, places: (c, 0, 0)),
                 pl.BlockSpec((1, cell_nodes, cell_nodes), lambda q, c, places: (c, 0, 0)),
             ],
-            out_specs=pl.BlockSpec((ext_count, CHUNK), lambda q, c, places: (0, q)),
+            out_specs=(
+                pl.BlockSpec((ext_count, CHUNK), lambda q, c, places: (0, 0)),
+                pl.BlockSpec((ext_count, CHUNK), lambda q, c, places: (0, jnp.maximum(q - 1, 0))),
+            ),
             scratch_shapes=[
                 pltpu.VMEM((ext_count * PITCH, LANES), jnp.float32),
                 pltpu.VMEM((cell_nodes * PITCH, LANES), jnp.float32),
@@ -266,8 +282,6 @@
     slab = lax.axis_index("slab")
     even = slab % 2 == 0
 
-    gathered = lax.all_gather(orbitals.astype(jnp.bfloat16), "orb", axis=0, tiled=True)
-
     has_lower = slab > 0
     has_upper = slab < slabs - 1
     has_a = jnp.where(even, has_upper, has_lower)
@@ -294,8 +308,9 @@
     own_columns = jnp.arange(own_count, dtype=jnp.int32) + face
 
     nodes = jnp.broadcast_to(connectivity[:, :, None], connectivity.shape + (LANES,))
-    shared_matrix = assemble(places, shared_columns, nodes, cell_matrices, ext_count)
-    own_matrix = assemble(places, own_columns, nodes, cell_matrices, ext_count)
+    shared_matrix, own_matrix = assemble(
+        places, jnp.concatenate([shared_columns, own_columns]), nodes, cell_matrices, ext_count
+    )
 
     face_nodes = jnp.concatenate([face_a, face_b])
     face_table = (
@@ -325,17 +340,26 @@
     def extend(own, at_a, at_b):
         return jnp.concatenate([own, at_a, at_b], axis=1).astype(jnp.bfloat16)
 
+    rounded = orbitals.astype(jnp.bfloat16)
     faces = lax.dot_general(
-        gathered, face_table, (((1,), (1,)), ((), ())), preferred_element_type=jnp.float32
+        rounded, face_table, (((1,), (1,)), ((), ())), preferred_element_type=jnp.float32
     ).astype(jnp.bfloat16)
     ghosts_a = lax.ppermute(faces[:, :face], "slab", pairs_a)
     ghosts_b = lax.ppermute(faces[:, face:], "slab", pairs_b)
-    start = jnp.concatenate([gathered, ghosts_a, ghosts_b], axis=1)
-    previous = tuple(x.astype(jnp.float32) for x in (gathered, ghosts_a, ghosts_b))
+    start = lax.all_gather(
+        jnp.concatenate([rounded, ghosts_a, ghosts_b], axis=1), "orb", axis=0, tiled=True
+    )
+    previous = (
+        start[:, :own_count],
+        start[:, own_count : own_count + face],
+        start[:, own_count + face :],
+    )
     current = apply_hamiltonian(start)
     for degree_step in range(1, DEGREE):
         product = apply_hamiltonian(extend(*current))
-        following = tuple(2.0 * p - q for p, q in zip(product, previous))
+        following = tuple(
+            2.0 * p - q.astype(jnp.float32) for p, q in zip(product, previous)
+        )
         previous, current = current, following
 
     filtered = current[0].astype(jnp.bfloat16)

time: 172 us -> 161 us (0.936)
  waiting for transfers between devices: 19.2 us -> 9.13 us
  starting transfers between devices: 36.3 us -> 43.6 us
  local copies, waits for them, and re-layouts: 4.8 us -> 0.87 us
  other arithmetic: 6.25 us -> 3.75 us
  Pallas kernels: 61.6 us -> 59.6 us
    ppermute x4, starting transfers between devices: 17.4 us -> 28.7 us  [apply_hamiltonian(): got_a = lax.ppermute(sent[:, :2 * face], 'slab', pairs_a)]
    all_gather x1, waiting for transfers between devices: 10.2 us -> 0.01 us  [per_device(): lax.all_gather(jnp.concatenate([rounded, ghosts_a, ghosts_b], axis=1), 'o...]
    another operation x3, other arithmetic: 2.91 us -> 0.41 us
    ppermute x1, starting transfers between devices: 2.89 us -> 0.52 us  [per_device(): ghosts_a = lax.ppermute(faces[:, :face], 'slab', pairs_a)]
    pallas_call x2 -> x1, Pallas kernels: 51.5 us -> 49.5 us  [assemble(): pl.pallas_call(assemble_kernel, out_shape=(jax.ShapeDtypeStruct((ext_coun...]
    dot_general x12, matrix products: 26.9 us -> 28.6 us  [times(): return jnp.dot(left, right, preferred_element_type=jnp.float32)]
  transfers between devices with their start and end apart: 14 -> 14, of which waited for: 5 -> 5; matrix products, arithmetic and copies ran while one was open for 7% -> 6% of each run, Pallas kernels for 30% -> 31%
where the time goes in v3:
time: 161 us
  Pallas kernels  59.6 us (37%)
  starting transfers between devices  43.6 us (27%)
  matrix products  30 us (19%)
  between operations  13.9 us (9%)
  waiting for transfers between devices  9.13 us (6%)
  other arithmetic  3.75 us (2%)
    pallas_call x1, Pallas kernels, assemble(): pl.pallas_call(assemble_kernel, out_shape=(jax.ShapeDtypeStruct((ext_coun...  49.5 us
    ppermute x4, starting transfers between devices, apply_hamiltonian(): got_a = lax.ppermute(sent[:, :2 * face], 'slab', pairs_a)  28.7 us
    dot_general x12, matrix products, times(): return jnp.dot(left, right, preferred_element_type=jnp.float32)  28.6 us
    ppermute x3, starting transfers between devices, sum_over(): got = lax.ppermute(sent, axis, [(i, i ^ step) for i in range(count)])  10.7 us
    pallas_call x1, Pallas kernels, orthonormal(): pl.pallas_call(functools.partial(orthonormal_kernel, scale), out_shape=ja...  10.1 us
    ppermute x3, waiting for transfers between devices, sum_over(): got = lax.ppermute(sent, axis, [(i, i ^ step) for i in range(count)])  8.41 us
  transfers between devices with their start and end apart: 14, of which 5 were waited for; matrix products, arithmetic and copies ran while one was open for 6% of the time, Pallas kernels for 31%

profile of v3, /device:TPU:0, one launch (start us, length us, event | category | flops | bytes accessed | tf_op | source)
XLA Modules:
  0.0 160.9 jit_solution(16502257016955190728)
XLA Ops:
  6.5 0.7 constant_dynamic-update-slice_fusion.2
  7.3 0.7 constant_dynamic-update-slice_fusion
  8.0 1.1 convert_element_type.82
  9.0 0.9 fusion.22
  11.4 0.7 pad_maximum_fusion.9
  12.8 49.5 %shard_map.55 = (bf16[2560,1024]{1,0:T(8,128)(2,1)}, bf16[2560,2048]{1,0:T(8,128)(2,1)}) custom-call(s32[4096]{0:T(1024)S(1)} %bitcast.20, s32[1,3072]{1,0:T(1,128)S(1)} %bitcast.21, s32[8,512,128]{2,1,0:T(8,128)S(1)} %broadcast_in_dim.20.nodes_ref, bf16[8,512,512]{2,1,0:T(8,128)(2,1)} %cell_ref.1), custom_call_target="tpu_custom_call" | custom-call | flops 12884901888 | bytes 28311552 | tf_op jit(solution)/shard_map/pallas_call | solution.py:121
  62.3 4.4 %fusion.75 = (bf16[256,1024]{1,0:T(8,128)(2,1)S(1)}, f32[256,1024]{1,0:T(8,128)S(1)}) fusion(bf16[256,2560]{1,0:T(8,128)(2,1)} %all-gather.2.cloned.1.call-done, bf16[2560,1024]{1,0:T(8,128)(2,1)} %get-tuple-element.8), kind=kOutput, calls=%fused_computation.102 | convolution fusion | flops 1342439424 | bytes 8126464 | tf_op jit(solution)/shard_map/dot_general | solution.py:324
  66.8 5.3 %collective-permute-start.2 = (bf16[256,512]{1,0:T(8,128)(2,1)S(1)}, bf16[256,512]{1,0:T(8,128)(2,1)S(1)}, u32[]{:S(2)}, u32[]{:S(2)}) collective-permute-start(bf16[256,512]{1,0:T(8,128)(2,1)S(1)} %get-tuple-element.25), channel_id=1, source_target_pairs={{0,4},{4,0},{8,12},{12,8},{16,20},{20,16},{24,28},{28,24},{1,5},{5... | collective-permute-start | bytes 786440 | tf_op jit(solution)/shard_map/ppermute | solution.py:329
  73.3 1.0 fusion.3
  74.4 6.3 %fusion.76 = (bf16[256,2048]{1,0:T(8,128)(2,1)S(1)}, f32[256,2048]{1,0:T(8,128)S(1)}) fusion(f32[256,2048]{1,0:T(8,128)S(1)} %fusion.3, bf16[256,2560]{1,0:T(8,128)(2,1)S(1)} %copy-done, bf16[2560,2048]{1,0:T(8,128)(2,1)} %get-tuple-element.7), kind=kOutput, calls=%fused_computation.103 | convolution fusion | flops 2685403136 | bytes 17039360 | tf_op jit(solution)/shard_map/dot_general | solution.py:324
  80.8 1.5 fusion.77
  82.4 10.2 %collective-permute-start.4 = (bf16[256,512]{1,0:T(8,128)(2,1)S(1)}, bf16[256,512]{1,0:T(8,128)(2,1)S(1)}, u32[]{:S(2)}, u32[]{:S(2)}) collective-permute-start(bf16[256,512]{1,0:T(8,128)(2,1)S(1)} %get-tuple-element.23), channel_id=1, source_target_pairs={{0,4},{4,0},{8,12},{12,8},{16,20},{20,16},{24,28},{28,24},{1,5},{5... | collective-permute-start | bytes 786440 | tf_op jit(solution)/shard_map/ppermute | solution.py:329
  92.6 0.8 collective-permute-start.5
  93.5 2.9 %fusion.27 = f32[256,2048]{1,0:T(8,128)S(1)} fusion(bf16[2560,2048]{1,0:T(8,128)(2,1)S(1)} %bitcast.25, bf16[256,256]{1,0:T(8,128)(2,1)S(1)} %get-tuple-element.18, bf16[256,256]{1,0:T(8,128)(2,1)S(1)} %get-tuple-element.17, bf16[256,2048]{1,0:T(8,128)(2,1)S(1)} %get-tuple-element.31), kind=kOutput, calls=%fused_computation.34 | convolution fusion | flops 2688286720 | bytes 13893632 | tf_op jit(solution)/shard_map/dot_general | solution.py:324
  96.6 1.3 fusion.78
  97.9 1.5 fusion.79
  99.4 5.4 %collective-permute-start.6 = (bf16[256,512]{1,0:T(8,128)(2,1)S(1)}, bf16[256,512]{1,0:T(8,128)(2,1)S(1)}, u32[]{:S(2)}, u32[]{:S(2)}) collective-permute-start(bf16[256,512]{1,0:T(8,128)(2,1)S(1)} %get-tuple-element.21), channel_id=1, source_target_pairs={{0,4},{4,0},{8,12},{12,8},{16,20},{20,16},{24,28},{28,24},{1,5},{5... | collective-permute-start | bytes 786440 | tf_op jit(solution)/shard_map/ppermute | solution.py:329
  104.8 0.7 collective-permute-start.7
  105.5 2.9 %fusion.25 = f32[256,2048]{1,0:T(8,128)S(1)} fusion(bf16[2560,2048]{1,0:T(8,128)(2,1)S(1)} %bitcast.25, bf16[256,256]{1,0:T(8,128)(2,1)S(1)} %get-tuple-element.14, bf16[256,256]{1,0:T(8,128)(2,1)S(1)} %get-tuple-element.13, bf16[256,2048]{1,0:T(8,128)(2,1)S(1)} %get-tuple-element.35), kind=kOutput, calls=%fused_computation.32 | convolution fusion | flops 2688286720 | bytes 13893632 | tf_op jit(solution)/shard_map/dot_general | solution.py:324
  108.4 1.2 fusion.14
  109.8 1.5 convolution_convert_fusion
  111.4 7.8 %collective-permute-start.8 = (bf16[256,512]{1,0:T(8,128)(2,1)S(1)}, bf16[256,512]{1,0:T(8,128)(2,1)S(1)}, u32[]{:S(2)}, u32[]{:S(2)}) collective-permute-start(bf16[256,512]{1,0:T(8,128)(2,1)S(1)} %get-tuple-element.19), channel_id=1, source_target_pairs={{0,4},{4,0},{8,12},{12,8},{16,20},{20,16},{24,28},{28,24},{1,5},{5... | collective-permute-start | bytes 786440 | tf_op jit(solution)/shard_map/ppermute | solution.py:329
  119.2 0.9 collective-permute-start.9
  120.1 2.9 %fusion.23 = f32[256,2048]{1,0:T(8,128)S(1)} fusion(bf16[2560,2048]{1,0:T(8,128)(2,1)S(1)} %bitcast.25, bf16[256,256]{1,0:T(8,128)(2,1)S(1)} %get-tuple-element.16, bf16[256,256]{1,0:T(8,128)(2,1)S(1)} %get-tuple-element.15, bf16[256,2048]{1,0:T(8,128)(2,1)S(1)} %fusion.14), kind=kOutput, calls=%fused_computation.30 | convolution fusion | flops 2688286720 | bytes 13893632 | tf_op jit(solution)/shard_map/dot_general | solution.py:324
  123.0 1.2 fusion.15.filtered_ref
  124.7 5.6 %collective-permute-start.10 = (bf16[256,256]{1,0:T(8,128)(2,1)S(1)}, bf16[256,256]{1,0:T(8,128)(2,1)S(1)}, u32[]{:S(2)}, u32[]{:S(2)}) collective-permute-start(bf16[256,256]{1,0:T(8,128)(2,1)S(1)} %convolution_convert_fusion.1), channel_id=1, source_target_pairs={{0,4},{4,0},{8,12},{12,8},{16,20},{20,16},{24,28},{28,24},{1,5},{5... | collective-permute-start | bytes 393224 | tf_op jit(solution)/shard_map/ppermute | solution.py:271
  130.3 1.0 collective-permute-done.10
  131.4 3.3 %collective-permute-start.11 = (bf16[256,256]{1,0:T(8,128)(2,1)S(1)}, bf16[256,256]{1,0:T(8,128)(2,1)S(1)}, u32[]{:S(2)}, u32[]{:S(2)}) collective-permute-start(bf16[256,256]{1,0:T(8,128)(2,1)S(1)} %add_convert_fusion.1), channel_id=1, source_target_pairs={{0,8},{4,12},{8,0},{12,4},{16,24},{20,28},{24,16},{28,20},{1,9},{5... | collective-permute-start | bytes 393224 | tf_op jit(solution)/shard_map/ppermute | solution.py:271
  134.6 4.0 %collective-permute-done.11 = bf16[256,256]{1,0:T(8,128)(2,1)S(1)} collective-permute-done((bf16[256,256]{1,0:T(8,128)(2,1)S(1)}, bf16[256,256]{1,0:T(8,128)(2,1)S(1)}, u32[]{:S(2)}, u32[]{:S(2)}) %collective-permute-start.11) | collective-permute-done | bytes 131104 | tf_op jit(solution)/shard_map/ppermute | solution.py:271
  138.7 1.8 %collective-permute-start.12 = (bf16[256,256]{1,0:T(8,128)(2,1)S(1)}, bf16[256,256]{1,0:T(8,128)(2,1)S(1)}, u32[]{:S(2)}, u32[]{:S(2)}) collective-permute-start(bf16[256,256]{1,0:T(8,128)(2,1)S(1)} %add_convert_fusion), channel_id=1, source_target_pairs={{0,16},{4,20},{8,24},{12,28},{16,0},{20,4},{24,8},{28,12},{1,17},{... | collective-permute-start | bytes 393224 | tf_op jit(solution)/shard_map/ppermute | solution.py:271
  140.5 3.4 %collective-permute-done.12 = bf16[256,256]{1,0:T(8,128)(2,1)S(1)} collective-permute-done((bf16[256,256]{1,0:T(8,128)(2,1)S(1)}, bf16[256,256]{1,0:T(8,128)(2,1)S(1)}, u32[]{:S(2)}, u32[]{:S(2)}) %collective-permute-start.12) | collective-permute-done | bytes 131104 | tf_op jit(solution)/shard_map/ppermute | solution.py:271
  144.0 10.1 %shard_map.56 = f32[64,2048]{1,0:T(8,128)} custom-call(s32[1]{0:T(128)} %bitcast.block_ref, f32[256,256]{1,0:T(8,128)S(1)} %convert_add_fusion.gram_ref, bf16[256,2048]{1,0:T(8,128)(2,1)S(1)} %fusion.15.filtered_ref), custom_call_target="tpu_custom_call" | custom-call | tf_op jit(solution)/shard_map/pallas_call | solution.py:243
  (60 shorter events, 4.4 us)
Async XLA Ops:
  6.5 5.6 %copy-start.1 = (s32[8,512]{1,0:T(8,128)S(1)}, s32[8,512]{1,0:T(8,128)}, u32[]{:S(2)}) copy-start(s32[8,512]{1,0:T(8,128)} %param.7) | copy-start | bytes 49156
  6.5 55.8 %all-gather.2.cloned.1.call-start = ((), (), s32[]{:S(2)}) async-start(), calls=%async_computation | async-start | bytes 1638400 | tf_op jit(solution)/shard_map/all_gather | solution.py:349
  10.0 1.4 collective-permute-start
  10.5 0.9 collective-permute-start.1
  66.7 7.6 %copy-start = (bf16[256,2560]{1,0:T(8,128)(2,1)S(1)}, bf16[256,2560]{1,0:T(8,128)(2,1)}, u32[]{:S(2)}) copy-start(bf16[256,2560]{1,0:T(8,128)(2,1)} %all-gather.2.cloned.1.call-done) | copy-start | bytes 3932164
  66.8 6.5 %collective-permute-start.2 = (bf16[256,512]{1,0:T(8,128)(2,1)S(1)}, bf16[256,512]{1,0:T(8,128)(2,1)S(1)}, u32[]{:S(2)}, u32[]{:S(2)}) collective-permute-start(bf16[256,512]{1,0:T(8,128)(2,1)S(1)} %get-tuple-element.25), channel_id=1, source_target_pairs={{0,4},{4,0},{8,12},{12,8},{16,20},{20,16},{24,28},{28,24},{1,5},{5... | collective-permute-start | bytes 786440 | tf_op jit(solution)/shard_map/ppermute | solution.py:329
  72.1 1.2 collective-permute-start.3
  73.3 7.5 %slice-start = ((s8[5242880]{0:T(1024)(128)(4,1)}), s8[4194304]{0:T(1024)(128)(4,1)S(1)}, s32[]{:S(2)}) async-start(s8[5242880]{0:T(1024)(128)(4,1)} %bitcast.22), calls=%async_computation.1 | async-start | bytes 8388608
  73.3 20.2 %slice-start.2 = ((s8[10485760]{0:T(1024)(128)(4,1)}), s8[4194304]{0:T(1024)(128)(4,1)S(1)}, s32[]{:S(2)}) async-start(s8[10485760]{0:T(1024)(128)(4,1)} %bitcast.24), calls=%async_computation.3 | async-start | bytes 8388608
  74.4 6.5 %slice-start.1 = ((s8[5242880]{0:T(1024)(128)(4,1)}), s8[1048576]{0:T(1024)(128)(4,1)S(1)}, s32[]{:S(2)}) async-start(s8[5242880]{0:T(1024)(128)(4,1)} %bitcast.22), calls=%async_computation.2 | async-start | bytes 2097152
  74.4 19.1 %slice-start.3 = ((s8[10485760]{0:T(1024)(128)(4,1)}), s8[4194304]{0:T(1024)(128)(4,1)S(1)}, s32[]{:S(2)}) async-start(s8[10485760]{0:T(1024)(128)(4,1)} %bitcast.24), calls=%async_computation.4 | async-start | bytes 8388608
  74.4 19.1 %slice-start.4 = ((s8[10485760]{0:T(1024)(128)(4,1)}), s8[2097152]{0:T(1024)(128)(4,1)S(1)}, s32[]{:S(2)}) async-start(s8[10485760]{0:T(1024)(128)(4,1)} %bitcast.24), calls=%async_computation.5 | async-start | bytes 4194304
  82.4 14.0 %collective-permute-start.4 = (bf16[256,512]{1,0:T(8,128)(2,1)S(1)}, bf16[256,512]{1,0:T(8,128)(2,1)S(1)}, u32[]{:S(2)}, u32[]{:S(2)}) collective-permute-start(bf16[256,512]{1,0:T(8,128)(2,1)S(1)} %get-tuple-element.23), channel_id=1, source_target_pairs={{0,4},{4,0},{8,12},{12,8},{16,20},{20,16},{24,28},{28,24},{1,5},{5... | collective-permute-start | bytes 786440 | tf_op jit(solution)/shard_map/ppermute | solution.py:329
  92.6 3.8 %collective-permute-start.5 = (bf16[256,512]{1,0:T(8,128)(2,1)S(1)}, bf16[256,512]{1,0:T(8,128)(2,1)S(1)}, u32[]{:S(2)}, u32[]{:S(2)}) collective-permute-start(bf16[256,512]{1,0:T(8,128)(2,1)S(1)} %get-tuple-element.24), channel_id=1, source_target_pairs={{4,8},{8,4},{12,16},{16,12},{20,24},{24,20},{5,9},{9,5},{13,17},{1... | collective-permute-start | bytes 786440 | tf_op jit(solution)/shard_map/ppermute | solution.py:330
  99.4 8.9 %collective-permute-start.6 = (bf16[256,512]{1,0:T(8,128)(2,1)S(1)}, bf16[256,512]{1,0:T(8,128)(2,1)S(1)}, u32[]{:S(2)}, u32[]{:S(2)}) collective-permute-start(bf16[256,512]{1,0:T(8,128)(2,1)S(1)} %get-tuple-element.21), channel_id=1, source_target_pairs={{0,4},{4,0},{8,12},{12,8},{16,20},{20,16},{24,28},{28,24},{1,5},{5... | collective-permute-start | bytes 786440 | tf_op jit(solution)/shard_map/ppermute | solution.py:329
  104.8 3.6 %collective-permute-start.7 = (bf16[256,512]{1,0:T(8,128)(2,1)S(1)}, bf16[256,512]{1,0:T(8,128)(2,1)S(1)}, u32[]{:S(2)}, u32[]{:S(2)}) collective-permute-start(bf16[256,512]{1,0:T(8,128)(2,1)S(1)} %get-tuple-element.22), channel_id=1, source_target_pairs={{4,8},{8,4},{12,16},{16,12},{20,24},{24,20},{5,9},{9,5},{13,17},{1... | collective-permute-start | bytes 786440 | tf_op jit(solution)/shard_map/ppermute | solution.py:330
  111.4 11.5 %collective-permute-start.8 = (bf16[256,512]{1,0:T(8,128)(2,1)S(1)}, bf16[256,512]{1,0:T(8,128)(2,1)S(1)}, u32[]{:S(2)}, u32[]{:S(2)}) collective-permute-start(bf16[256,512]{1,0:T(8,128)(2,1)S(1)} %get-tuple-element.19), channel_id=1, source_target_pairs={{0,4},{4,0},{8,12},{12,8},{16,20},{20,16},{24,28},{28,24},{1,5},{5... | collective-permute-start | bytes 786440 | tf_op jit(solution)/shard_map/ppermute | solution.py:329
  119.2 3.8 %collective-permute-start.9 = (bf16[256,512]{1,0:T(8,128)(2,1)S(1)}, bf16[256,512]{1,0:T(8,128)(2,1)S(1)}, u32[]{:S(2)}, u32[]{:S(2)}) collective-permute-start(bf16[256,512]{1,0:T(8,128)(2,1)S(1)} %get-tuple-element.20), channel_id=1, source_target_pairs={{4,8},{8,4},{12,16},{16,12},{20,24},{24,20},{5,9},{9,5},{13,17},{1... | collective-permute-start | bytes 786440 | tf_op jit(solution)/shard_map/ppermute | solution.py:330
  124.7 6.6 %collective-permute-start.10 = (bf16[256,256]{1,0:T(8,128)(2,1)S(1)}, bf16[256,256]{1,0:T(8,128)(2,1)S(1)}, u32[]{:S(2)}, u32[]{:S(2)}) collective-permute-start(bf16[256,256]{1,0:T(8,128)(2,1)S(1)} %convolution_convert_fusion.1), channel_id=1, source_target_pairs={{0,4},{4,0},{8,12},{12,8},{16,20},{20,16},{24,28},{28,24},{1,5},{5... | collective-permute-start | bytes 393224 | tf_op jit(solution)/shard_map/ppermute | solution.py:271
  131.4 7.3 %collective-permute-start.11 = (bf16[256,256]{1,0:T(8,128)(2,1)S(1)}, bf16[256,256]{1,0:T(8,128)(2,1)S(1)}, u32[]{:S(2)}, u32[]{:S(2)}) collective-permute-start(bf16[256,256]{1,0:T(8,128)(2,1)S(1)} %add_convert_fusion.1), channel_id=1, source_target_pairs={{0,8},{4,12},{8,0},{12,4},{16,24},{20,28},{24,16},{28,20},{1,9},{5... | collective-permute-start | bytes 393224 | tf_op jit(solution)/shard_map/ppermute | solution.py:271
  138.7 5.3 %collective-permute-start.12 = (bf16[256,256]{1,0:T(8,128)(2,1)S(1)}, bf16[256,256]{1,0:T(8,128)(2,1)S(1)}, u32[]{:S(2)}, u32[]{:S(2)}) collective-permute-start(bf16[256,256]{1,0:T(8,128)(2,1)S(1)} %add_convert_fusion), channel_id=1, source_target_pairs={{0,16},{4,20},{8,24},{12,28},{16,0},{20,4},{24,8},{28,12},{1,17},{... | collective-permute-start | bytes 393224 | tf_op jit(solution)/shard_map/ppermute | solution.py:271
Sparse Core Ops, SparseCore 0:
  12.3 39.3 all-gather.1
